TPU v7x, 32 devices: a whole 2x2x4 slice. The times are simulated.
32 devices in a mesh: section: 2 (over core), dp: 4 (over z), ctx: 4 (over y, x).
Axes of the slice: x: 2, y: 2, z: 4, core: 2. Of those that a mesh axis runs over, the one named last changes fastest.
Arguments:
- ends: bfloat16 [2, 2, 3584, 960], P('section', None, ('dp', 'ctx')), may hold values from -6 to 6
- doc_lengths: int32 [2, 4, 2], P(None, 'dp'), may hold values from 0 to 896, as said below
- w_query: bfloat16 [960, 960], replicated, may hold values from -0.1875 to 0.1875
- key_projection_weight: bfloat16 [960, 320], replicated, may hold values from -0.1875 to 0.1875
- value_projection_weight: bfloat16 [960, 320], replicated, may hold values from -0.1875 to 0.1875
- w_out: bfloat16 [960, 960], replicated, may hold values from -0.75 to 0.75
- w_gate: bfloat16 [960, 2560], replicated, may hold values from -0.1875 to 0.1875
- w_up: bfloat16 [960, 2560], replicated, may hold values from -0.1875 to 0.1875
- w_down: bfloat16 [2560, 960], replicated, may hold values from -0.125 to 0.125
- gain_attn: bfloat16 [960], replicated, may hold values from 0.5 to 1.5
- gain_ffn: bfloat16 [960], replicated, may hold values from 0.5 to 1.5
Outputs:
- acts: bfloat16 [2, 2, 3584, 960], P('section', None, ('dp', 'ctx'))
- grads_in: bfloat16 [2, 2, 3584, 960], P('section', None, ('dp', 'ctx'))
- grad_w_query: float32 [960, 960], P('dp')
- grad_w_key: float32 [960, 320], P('dp')
- grad_w_value: float32 [960, 320], P('dp')
- grad_w_out: float32 [960, 960], P('dp')
- grad_w_gate: float32 [960, 2560], P('dp')
- grad_w_up: float32 [960, 2560], P('dp')
- grad_w_down: float32 [2560, 960], P('dp')
- grad_gain_attn: float32 [960], P('dp')
- grad_gain_ffn: float32 [960], P('dp')
Inputs may be any that keep to these rules, and one draw needn't show every extreme that they name: `doc_lengths`: each row holds either one sequence of 896 tokens followed by an empty slot, or a sequence of 512 tokens followed by one of 384. Of the two micro-batches' rows at the same index of dimension 1, exactly one holds the single sequence.
All inputs are finite; a program needn't handle non-finite values.
Results may differ from a plain program's by a relative error of at most 0.028.
Values may be sent and summed in bfloat16 or wider, within the bound.
A program may use at most 192 MiB of HBM per device.

v0:
```python
import jax
import jax.numpy as jnp
from jax import lax
from jax.sharding import PartitionSpec as P

QUERY_HEADS = 15
KEY_VALUE_HEADS = 5
HEAD_SIZE = 64


epsilon = 1e-05
masked_fill = -1e30


def from_behind(array, axis, by):
    devices = lax.axis_size(axis)
    pairs = [(i, i + by) for i in range(devices) if 0 <= i + by < devices]
    return lax.ppermute(array, axis, pairs)


def as_sent(array):
    return jax.tree.map(lambda a: a.astype(jnp.bfloat16) if a.dtype == jnp.float32 else a, array)


def positions(lengths, grouped_row_block):
    finish = jnp.cumsum(lengths)
    token_index = jnp.arange(grouped_row_block, dtype=jnp.int32)
    passed = (token_index[:, None] >= finish[None, :]).astype(jnp.int32)
    segment = jnp.sum(passed, axis=1)
    token_position = token_index - jnp.sum(passed * lengths[None, :], axis=1)
    return (segment, token_position)


def rotary_embed(heads, token_position, direction):
    half_width = heads.shape[-1] // 2
    frequency = 10000.0 ** (-2.0 * jnp.arange(half_width, dtype=jnp.float32) / heads.shape[-1])
    angles = token_position.astype(jnp.float32)[:, None] * frequency[None, :]
    cosines = jnp.cos(angles)[:, None, :]
    sines = direction * jnp.sin(angles)[:, None, :]
    front_half = heads[..., :half_width]
    back_half = heads[..., half_width:]
    return jnp.concatenate(
        [front_half * cosines - back_half * sines, back_half * cosines + front_half * sines],
        axis=-1,
    )


def norm_rows(hidden, gain_vec):
    return (
        hidden * lax.rsqrt(jnp.mean(hidden * hidden, axis=-1, keepdims=True) + epsilon) * gain_vec
    )


def norm_back(hidden, gain_vec, upstream):
    scale = lax.rsqrt(jnp.mean(hidden * hidden, axis=-1, keepdims=True) + epsilon)
    weighted = upstream * gain_vec
    grad_rows = scale * weighted - hidden * scale**3 * jnp.mean(
        weighted * hidden, axis=-1, keepdims=True
    )
    grad_gain = jnp.sum(upstream * hidden * scale, axis=0)
    return (grad_rows, grad_gain)


def weighted_product(left, right):
    return jnp.dot(left, right, preferred_element_type=jnp.float32)


def product_back(left, right):
    return lax.dot_general(
        left, right, (((1,), (1,)), ((), ())), preferred_element_type=jnp.float32
    )


def outer_sum(left, right):
    return lax.dot_general(
        left, right, (((0,), (0,)), ((), ())), preferred_element_type=jnp.float32
    )


def allowed_mask(segment_all, segment_mine, offset):
    device_rows = segment_mine.shape[0]
    query_index = offset + jnp.arange(device_rows, dtype=jnp.int32)
    key_index = jnp.arange(segment_all.shape[0], dtype=jnp.int32)
    return (segment_mine[:, None] == segment_all[None, :]) & (
        query_index[:, None] >= key_index[None, :]
    )


def scores_of(query_rows, gathered_keys, allowed):
    device_rows = query_rows.shape[0]
    query_groups = query_rows.reshape(
        device_rows, KEY_VALUE_HEADS, QUERY_HEADS // KEY_VALUE_HEADS, HEAD_SIZE
    )
    key_head_rows = gathered_keys.reshape(gathered_keys.shape[0], KEY_VALUE_HEADS, HEAD_SIZE)
    raw_scores = (
        jnp.einsum(
            "qkgd,skd->kgqs", query_groups, key_head_rows, preferred_element_type=jnp.float32
        )
        * 0.125
    )
    return jnp.where(allowed[None, None], raw_scores, masked_fill)


def pick(layouts, micro_index, offset):
    return tuple(
        (lax.dynamic_index_in_dim(part, micro_index, 0, keepdims=False) for part in layouts)
    ) + (offset,)


def forward_layer(start_rows, weights, gains, layout):
    w_query, key_projection_weight, value_projection_weight, w_out, w_gate, w_up, w_down = weights
    gain_attn, gain_ffn = gains
    segment_all, segment_mine, device_token_position, offset = layout
    device_rows = start_rows.shape[0]
    hidden_in = start_rows.astype(jnp.float32)
    normalized_input = norm_rows(hidden_in, gain_attn).astype(jnp.bfloat16)
    query_rows = (
        rotary_embed(
            weighted_product(normalized_input, w_query).reshape(
                device_rows, QUERY_HEADS, HEAD_SIZE
            ),
            device_token_position,
            1.0,
        )
        .astype(jnp.bfloat16)
        .reshape(device_rows, QUERY_HEADS * HEAD_SIZE)
    )
    key_local = (
        rotary_embed(
            weighted_product(normalized_input, key_projection_weight).reshape(
                device_rows, KEY_VALUE_HEADS, HEAD_SIZE
            ),
            device_token_position,
            1.0,
        )
        .astype(jnp.bfloat16)
        .reshape(device_rows, KEY_VALUE_HEADS * HEAD_SIZE)
    )
    value_local = weighted_product(normalized_input, value_projection_weight).astype(jnp.bfloat16)
    gathered_keys, gathered_values = (
        lax.all_gather(key_local, "ctx", axis=0, tiled=True),
        lax.all_gather(value_local, "ctx", axis=0, tiled=True),
    )
    grouped_row_block = gathered_keys.shape[0]
    allowed = allowed_mask(segment_all, segment_mine, offset)
    scores = scores_of(query_rows, gathered_keys, allowed)
    row_peak = jnp.max(scores, axis=-1, keepdims=True)
    exponent = jnp.exp(scores - row_peak)
    row_total = jnp.sum(exponent, axis=-1, keepdims=True)
    soft_probs = (exponent / row_total).astype(jnp.bfloat16)
    log_total = row_peak + jnp.log(row_total)
    mixed_heads = jnp.einsum(
        "kgqs,skd->qkgd",
        soft_probs,
        gathered_values.reshape(grouped_row_block, KEY_VALUE_HEADS, HEAD_SIZE),
        preferred_element_type=jnp.float32,
    )
    mixed_heads = mixed_heads.reshape(device_rows, QUERY_HEADS * HEAD_SIZE).astype(jnp.bfloat16)
    middle = hidden_in + weighted_product(mixed_heads, w_out)
    normed_ffn = norm_rows(middle, gain_ffn).astype(jnp.bfloat16)
    gate_act = weighted_product(normed_ffn, w_gate)
    up_act = weighted_product(normed_ffn, w_up)
    inner_act = (gate_act * jax.nn.sigmoid(gate_act) * up_act).astype(jnp.bfloat16)
    result = (middle + weighted_product(inner_act, w_down)).astype(jnp.bfloat16)
    key_part, value_part = (gathered_keys, gathered_values)
    stored = (
        start_rows,
        normalized_input,
        query_rows,
        key_part,
        value_part,
        log_total,
        mixed_heads,
        middle,
        normed_ffn,
        gate_act,
        up_act,
        inner_act,
    )
    return (result, stored)


def backward_layer(grad_out, stored, weights, gains, layout):
    w_query, key_projection_weight, value_projection_weight, w_out, w_gate, w_up, w_down = weights
    gain_attn, gain_ffn = gains
    segment_all, segment_mine, device_token_position, offset = layout
    (
        start_rows,
        normalized_input,
        query_rows,
        key_part,
        value_part,
        log_total,
        mixed_heads,
        middle,
        normed_ffn,
        gate_act,
        up_act,
        inner_act,
    ) = stored
    gathered_keys, gathered_values = (key_part, value_part)
    device_rows = start_rows.shape[0]
    grouped_row_block = gathered_keys.shape[0]
    hidden_in = start_rows.astype(jnp.float32)
    branch = grad_out.astype(jnp.bfloat16)
    grad_down = outer_sum(inner_act, branch)
    grad_inner = product_back(branch, w_down)
    sigmoid_gate = jax.nn.sigmoid(gate_act)
    grad_gate = (
        grad_inner * up_act * sigmoid_gate * (1.0 + gate_act * (1.0 - sigmoid_gate))
    ).astype(jnp.bfloat16)
    grad_upper = (grad_inner * gate_act * sigmoid_gate).astype(jnp.bfloat16)
    grad_w_gate = outer_sum(normed_ffn, grad_gate)
    grad_w_up = outer_sum(normed_ffn, grad_upper)
    grad_normed_ffn = product_back(grad_gate, w_gate) + product_back(grad_upper, w_up)
    grad_norm_ffn, grad_gain_ffn = norm_back(middle, gain_ffn, grad_normed_ffn)
    grad_middle = grad_out + grad_norm_ffn
    attn_branch = grad_middle.astype(jnp.bfloat16)
    grad_w_out = outer_sum(mixed_heads, attn_branch)
    grad_mixed = (
        product_back(attn_branch, w_out)
        .astype(jnp.bfloat16)
        .reshape(device_rows, KEY_VALUE_HEADS, QUERY_HEADS // KEY_VALUE_HEADS, HEAD_SIZE)
    )
    allowed = allowed_mask(segment_all, segment_mine, offset)
    value_head_rows = gathered_values.reshape(grouped_row_block, KEY_VALUE_HEADS, HEAD_SIZE)
    key_head_rows = gathered_keys.reshape(grouped_row_block, KEY_VALUE_HEADS, HEAD_SIZE)
    query_groups = query_rows.reshape(
        device_rows, KEY_VALUE_HEADS, QUERY_HEADS // KEY_VALUE_HEADS, HEAD_SIZE
    )
    query_parts, key_shard_list, value_shard_list = ([], [], [])
    for head_number in range(KEY_VALUE_HEADS):
        head_queries = query_groups[:, head_number]
        head_grad = grad_mixed[:, head_number]
        head_keys = key_head_rows[:, head_number]
        head_scores = (
            jnp.einsum("qgd,sd->gqs", head_queries, head_keys, preferred_element_type=jnp.float32)
            * 0.125
        )
        head_scores = jnp.where(allowed[None], head_scores, masked_fill)
        head_probs = jnp.exp(head_scores - log_total[head_number])
        grad_probs = jnp.einsum(
            "qgd,sd->gqs",
            head_grad,
            value_head_rows[:, head_number],
            preferred_element_type=jnp.float32,
        )
        row_weight = jnp.sum(head_probs * grad_probs, axis=-1, keepdims=True)
        grad_scores = (head_probs * (grad_probs - row_weight)).astype(jnp.bfloat16)
        value_shard_list.append(
            jnp.einsum(
                "gqs,qgd->sd",
                head_probs.astype(jnp.bfloat16),
                head_grad,
                preferred_element_type=jnp.float32,
            )
        )
        query_parts.append(
            jnp.einsum("gqs,sd->qgd", grad_scores, head_keys, preferred_element_type=jnp.float32)
            * 0.125
        )
        key_shard_list.append(
            jnp.einsum("gqs,qgd->sd", grad_scores, head_queries, preferred_element_type=jnp.float32)
            * 0.125
        )
    grad_query = jnp.stack(query_parts, axis=1)
    key_gradient_full = jnp.stack(key_shard_list, axis=1).reshape(
        grouped_row_block, KEY_VALUE_HEADS * HEAD_SIZE
    )
    value_gradient_full = jnp.stack(value_shard_list, axis=1).reshape(
        grouped_row_block, KEY_VALUE_HEADS * HEAD_SIZE
    )
    key_gradient, grad_value = (
        lax.psum_scatter(
            key_gradient_full.astype(jnp.bfloat16), "ctx", scatter_dimension=0, tiled=True
        ).astype(jnp.float32),
        lax.psum_scatter(
            value_gradient_full.astype(jnp.bfloat16), "ctx", scatter_dimension=0, tiled=True
        ).astype(jnp.float32),
    )
    grad_query = (
        rotary_embed(
            grad_query.reshape(device_rows, QUERY_HEADS, HEAD_SIZE), device_token_position, -1.0
        )
        .reshape(device_rows, QUERY_HEADS * HEAD_SIZE)
        .astype(jnp.bfloat16)
    )
    key_gradient = (
        rotary_embed(
            key_gradient.reshape(device_rows, KEY_VALUE_HEADS, HEAD_SIZE),
            device_token_position,
            -1.0,
        )
        .reshape(device_rows, KEY_VALUE_HEADS * HEAD_SIZE)
        .astype(jnp.bfloat16)
    )
    grad_value = grad_value.astype(jnp.bfloat16)
    grad_w_query = outer_sum(normalized_input, grad_query)
    grad_w_key = outer_sum(normalized_input, key_gradient)
    grad_w_value = outer_sum(normalized_input, grad_value)
    grad_normed = (
        product_back(grad_query, w_query)
        + product_back(key_gradient, key_projection_weight)
        + product_back(grad_value, value_projection_weight)
    )
    grad_norm_attn, grad_gain_attn = norm_back(hidden_in, gain_attn, grad_normed)
    grad_rows = grad_middle + grad_norm_attn
    return (
        grad_rows,
        (
            grad_w_query,
            grad_w_key,
            grad_w_value,
            grad_w_out,
            grad_w_gate,
            grad_w_up,
            grad_down,
            grad_gain_attn,
            grad_gain_ffn,
        ),
    )


def shards(
    ends,
    doc_lengths,
    w_query,
    key_projection_weight,
    value_projection_weight,
    w_out,
    w_gate,
    w_up,
    w_down,
    gain_attn,
    gain_ffn,
):
    weights = (w_query, key_projection_weight, value_projection_weight, w_out, w_gate, w_up, w_down)
    gains = (gain_attn.astype(jnp.float32), gain_ffn.astype(jnp.float32))
    section_index = lax.axis_index("section")
    micro_count = ends.shape[1]
    device_rows = ends.shape[2]
    grouped_row_block = device_rows * lax.axis_size("ctx")
    offset = lax.axis_index("ctx") * device_rows
    segment_rows, segment_local, position_local = ([], [], [])
    for micro_index in range(micro_count):
        segment, token_position = positions(doc_lengths[micro_index, 0], grouped_row_block)
        segment_rows.append(segment)
        segment_local.append(lax.dynamic_slice_in_dim(segment, offset, device_rows))
        position_local.append(lax.dynamic_slice_in_dim(token_position, offset, device_rows))
    layouts = (jnp.stack(segment_rows), jnp.stack(segment_local), jnp.stack(position_local))
    carried = jnp.zeros((device_rows, ends.shape[3]), jnp.bfloat16)
    results = []
    stored_all = []
    for period in range(micro_count + 1):
        micro_index = jnp.clip(period - section_index, 0, micro_count - 1)
        own_block = lax.dynamic_index_in_dim(ends[0], micro_index, 0, keepdims=False)
        start_rows = jnp.where(section_index == 0, own_block, carried)
        result, stored = forward_layer(
            start_rows, weights, gains, pick(layouts, micro_index, offset)
        )
        results.append(result)
        stored_all.append(stored)
        if period < micro_count:
            carried = from_behind(result, "section", 1)
    stacked = jax.tree.map(lambda *parts: jnp.stack(parts), *stored_all)
    returned = jnp.zeros((device_rows, ends.shape[3]), jnp.bfloat16)
    back_results = []
    summed = None
    for period in range(micro_count + 1):
        micro_raw = period - (1 - section_index)
        active = ((micro_raw >= 0) & (micro_raw < micro_count)).astype(jnp.float32)
        micro_index = jnp.clip(micro_raw, 0, micro_count - 1)
        own_block = lax.dynamic_index_in_dim(ends[0], micro_index, 0, keepdims=False)
        grad_out = jnp.where(section_index == 1, own_block, returned).astype(jnp.float32) * active
        stored = jax.tree.map(
            lambda part: lax.dynamic_index_in_dim(
                part, micro_index + section_index, 0, keepdims=False
            ),
            stacked,
        )
        grad_rows, grad_params = backward_layer(
            grad_out, stored, weights, gains, pick(layouts, micro_index, offset)
        )
        sent = grad_rows.astype(jnp.bfloat16)
        back_results.append(sent)
        if period < micro_count:
            returned = from_behind(sent, "section", -1)
        summed = grad_params if summed is None else jax.tree.map(jnp.add, summed, grad_params)
    summed = jax.tree.map(
        lambda part: part.astype(jnp.float32),
        lax.psum_scatter(as_sent(summed), "dp", scatter_dimension=0, tiled=True),
    )
    totals = jax.tree.map(
        lambda part: part.astype(jnp.float32), lax.psum(as_sent(summed), ("section", "ctx"))
    )
    forward_stack = jnp.stack(results)
    back_stack = jnp.stack(back_results)
    acts = jnp.stack(
        [
            lax.dynamic_index_in_dim(forward_stack, number + section_index, 0, keepdims=False)
            for number in range(micro_count)
        ]
    )[None]
    grads_in = jnp.stack(
        [
            lax.dynamic_index_in_dim(back_stack, number + 1 - section_index, 0, keepdims=False)
            for number in range(micro_count)
        ]
    )[None]
    return (acts, grads_in) + tuple(totals)


def solution(mesh):
    return jax.shard_map(
        shards,
        mesh=mesh,
        in_specs=(
            P("section", None, ("dp", "ctx"), None),
            P(None, "dp", None),
            P(),
            P(),
            P(),
            P(),
            P(),
            P(),
            P(),
            P(),
            P(),
        ),
        out_specs=(
            P("section", None, ("dp", "ctx"), None),
            P("section", None, ("dp", "ctx"), None),
            P("dp", None),
            P("dp", None),
            P("dp", None),
            P("dp", None),
            P("dp", None),
            P("dp", None),
            P("dp", None),
            P("dp"),
            P("dp"),
        ),
        check_vma=False,
    )
```

profile of v0, /device:TPU:0, one launch (start us, length us, event | category | flops | bytes accessed | tf_op | source)
XLA Modules:
  0.0 1063.3 jit_solution(16408104071356623331)
XLA Ops:
  25.4 12.0 %all-gather.1 = bf16[4,224,320]{1,2,0:T(8,128)(2,1)S(1)} all-gather(bf16[1,224,320]{1,2,0:T(8,128)(2,1)S(1)} %bitcast.1832), channel_id=1, replica_groups=mesh['section'=2,'dp'=4,'ctx'=4] {'ctx'}, dimensions={0}, use_global_device_ids=true | all-gather | bytes 716800 | tf_op jit(solution)/shard_map/all_gather | solution.py:141
  38.0 11.2 %all-gather = bf16[4,224,320]{1,2,0:T(8,128)(2,1)S(1)} all-gather(bf16[1,224,320]{1,2,0:T(8,128)(2,1)S(1)} %fusion.310), channel_id=1, replica_groups=mesh['section'=2,'dp'=4,'ctx'=4] {'ctx'}, dimensions={0}, use_global_device_ids=true | all-gather | bytes 716800 | tf_op jit(solution)/shard_map/all_gather | solution.py:142
  96.9 9.9 all-gather.2
  114.3 10.4 all-gather.3
  158.6 10.6 all-gather.4
  176.7 10.5 all-gather.5
  222.2 6.8 fusion.109
  230.6 4.8 fusion.488
  291.4 12.2 %reduce-scatter.40.cloned.1.call-done = bf16[224,320]{1,0:T(8,128)(2,1)} async-done(((bf16[896,320]{1,0:T(8,128)(2,1)}), bf16[224,320]{1,0:T(8,128)(2,1)}) %reduce-scatter.40.cloned.1.call-update) | async-done | bytes 143376
  308.3 24.0 %reduce-scatter.42.cloned.1.call-done = bf16[224,320]{1,0:T(8,128)(2,1)} async-done(((bf16[896,320]{1,0:T(8,128)(2,1)}), bf16[224,320]{1,0:T(8,128)(2,1)}) %reduce-scatter.42.cloned.1.call-update) | async-done | bytes 143376
  342.0 5.6 fusion.100
  393.2 9.3 reduce-scatter.44.cloned.1.call-done
  409.2 22.5 %reduce-scatter.46.cloned.1.call-done = bf16[224,320]{1,0:T(8,128)(2,1)} async-done(((bf16[896,320]{1,0:T(8,128)(2,1)}), bf16[224,320]{1,0:T(8,128)(2,1)}) %reduce-scatter.46.cloned.1.call-update) | async-done | bytes 143376
  440.0 5.6 fusion.91
  448.2 4.7 fusion.474
  499.2 5.2 reduce-scatter.50.cloned.1.call-done
  507.6 6.6 fusion.303
  516.0 17.0 %reduce-scatter.48.cloned.1.call-done = bf16[224,320]{1,0:T(8,128)(2,1)} async-done(((bf16[896,320]{1,0:T(8,128)(2,1)}), bf16[224,320]{1,0:T(8,128)(2,1)}) %reduce-scatter.48.cloned.1.call-update) | async-done | bytes 143376
  543.2 8.3 add_convert_fusion
  551.5 7.9 copy.126
  580.6 5.2 fusion.532
  585.8 7.9 add_convert_fusion.1
  596.6 5.2 fusion.534
  601.9 7.9 add_convert_fusion.2
  621.7 56.1 %reduce-scatter.56.cloned.1.call-done = bf16[640,960]{1,0:T(8,128)(2,1)} async-done(((bf16[2560,960]{1,0:T(8,128)(2,1)}), bf16[640,960]{1,0:T(8,128)(2,1)}) %reduce-scatter.56.cloned.1.call-update) | async-done | bytes 1228816
  680.2 42.3 %reduce-scatter.34.cloned.1.call-done = bf16[240,960]{1,0:T(8,128)(2,1)} async-done(((bf16[960,960]{1,0:T(8,128)(2,1)}), bf16[240,960]{1,0:T(8,128)(2,1)}) %reduce-scatter.34.cloned.1.call-update) | async-done | bytes 460816 | tf_op jit(solution)/shard_map/reduce_scatter | solution.py:391
  722.5 43.6 %reduce-scatter.32.cloned.1.call-done = bf16[240,960]{1,0:T(8,128)(2,1)} async-done(((bf16[960,960]{1,0:T(8,128)(2,1)}), bf16[240,960]{1,0:T(8,128)(2,1)}) %reduce-scatter.32.cloned.1.call-update) | async-done | bytes 460816 | tf_op jit(solution)/shard_map/reduce_scatter | solution.py:391
  766.1 89.9 %reduce-scatter.38.cloned.1.call-done = bf16[240,2560]{1,0:T(8,128)(2,1)} async-done(((bf16[960,2560]{1,0:T(8,128)(2,1)}), bf16[240,2560]{1,0:T(8,128)(2,1)}) %reduce-scatter.38.cloned.1.call-update) | async-done | bytes 1228816 | tf_op jit(solution)/shard_map/reduce_scatter | solution.py:391
  856.0 91.4 %reduce-scatter.36.cloned.1.call-done = bf16[240,2560]{1,0:T(8,128)(2,1)} async-done(((bf16[960,2560]{1,0:T(8,128)(2,1)}), bf16[240,2560]{1,0:T(8,128)(2,1)}) %reduce-scatter.36.cloned.1.call-update) | async-done | bytes 1228816 | tf_op jit(solution)/shard_map/reduce_scatter | solution.py:391
  952.7 11.0 %all-reduce.4 = (bf16[960]{0:T(1024)(128)(2,1)S(1)}, bf16[960]{0:T(1024)(128)(2,1)S(1)}) all-reduce(bf16[960]{0:T(1024)(128)(2,1)S(1)} %add_convert_fusion.12, bf16[960]{0:T(1024)(128)(2,1)S(1)} %add_convert_fusion.11), channel_id=15, replica_groups=mesh['section'=2,'dp'=4,'ctx'=4] {'dp'}, use_global_device_ids=true, to_apply=%region_68.69.clone | all-reduce | flops 1920 | bytes 7680
  963.8 15.8 %all-reduce.2 = (bf16[240]{0:T(256)(128)(2,1)S(1)}, bf16[240]{0:T(256)(128)(2,1)S(1)}) all-reduce(bf16[240]{0:T(256)(128)(2,1)S(1)} %dynamic-slice.7, bf16[240]{0:T(256)(128)(2,1)S(1)} %dynamic-slice.9), channel_id=1, replica_groups=mesh['section'=2,'dp'=4,'ctx'=4] {'section','ctx'}, use_global_device_ids=true, to_apply=%region_69.70 | all-reduce | flops 480 | bytes 1920 | tf_op jit(solution)/shard_map/psum | solution.py:394
  983.8 61.1 %all-reduce.7.cloned.1.call-done = (bf16[240,960]{1,0:T(8,128)(2,1)}, bf16[240,320]{0,1:T(8,128)(2,1)}, bf16[240,320]{0,1:T(8,128)(2,1)}, bf16[240,960]{1,0:T(8,...) async-done(((bf16[240,960]{1,0:T(8,128)(2,1)}, bf16[240,320]{0,1:T(8,128)(2,1)}, bf16[240,320]{0,1:T(8,128)(2,1)}, ...) | async-done | bytes 4915216 | tf_op jit(solution)/shard_map/psum | solution.py:394
  (836 shorter events, 402.8 us)
Async XLA Ops:
  7.2 65.8 %copy-start = (bf16[960,960]{1,0:T(8,128)(2,1)S(1)}, bf16[960,960]{1,0:T(8,128)(2,1)}, u32[]{:S(2)}) copy-start(bf16[960,960]{1,0:T(8,128)(2,1)} %param.16) | copy-start | bytes 5529604
  7.2 296.4 %reduce-scatter.40.cloned.1.call-start = ((), (), s32[]{:S(2)}) async-start(), calls=%async_computation.17 | async-start | bytes 860160
  81.4 12.6 %collective-permute-start = (bf16[224,960]{1,0:T(8,128)(2,1)}, bf16[224,960]{1,0:T(8,128)(2,1)}, u32[]{:S(2)}, u32[]{:S(2)}) collective-permute-start(bf16[224,960]{1,0:T(8,128)(2,1)} %fusion.116), channel_id=1, source_target_pairs={{0,16},{1,17},{2,18},{3,19},{4,20},{5,21},{6,22},{7,23},{8,24},{9,... | collective-permute-start | bytes 1290248 | tf_op jit(solution)/shard_map/ppermute | solution.py:18
  94.2 36.9 %copy-start.189 = (f32[224]{0:T(256)}, f32[224]{0:T(256)S(1)}, u32[]{:S(2)}) copy-start(f32[224]{0:T(256)S(1)} %add_rsqrt_fusion.9) | copy-start | bytes 2692
  151.5 4.9 collective-permute-start.1
  156.7 37.0 %copy-start.191 = (f32[224]{0:T(256)}, f32[224]{0:T(256)S(1)}, u32[]{:S(2)}) copy-start(f32[224]{0:T(256)S(1)} %add_rsqrt_fusion.7) | copy-start | bytes 2692
  158.6 17.0 %copy-start.154 = (f32[224,32]{0,1:T(8,128)S(1)}, f32[224,32]{0,1:T(8,128)}, u32[]{:S(2)}) copy-start(f32[224,32]{0,1:T(8,128)} %get-tuple-element.162) | copy-start | bytes 86020
  209.9 25.6 %copy-start.19 = (f32[3,224,960]{2,1,0:T(8,128)}, f32[3,224,960]{2,1,0:T(8,128)S(1)}, u32[]{:S(2)}) copy-start(f32[3,224,960]{2,1,0:T(8,128)S(1)} %pad_maximum_fusion.3) | copy-start | bytes 7741444
  277.6 54.7 %reduce-scatter.42.cloned.1.call-start = ((), (), s32[]{:S(2)}) async-start(), calls=%async_computation.18 | async-start | bytes 860160
  287.3 115.2 %reduce-scatter.44.cloned.1.call-start = ((), (), s32[]{:S(2)}) async-start(), calls=%async_computation.19 | async-start | bytes 860160
  305.5 26.9 %copy-start.193 = (f32[224]{0:T(256)S(1)}, f32[224]{0:T(256)}, u32[]{:S(2)}) copy-start(f32[224]{0:T(256)} %get-tuple-element.152) | copy-start | bytes 2692
  305.5 29.9 %copy-start.112 = (bf16[224,5,64]{0,2,1:T(8,128)(2,1)}, bf16[224,5,64]{0,2,1:T(8,128)(2,1)S(1)}, u32[]{:S(2)}) copy-start(bf16[224,5,64]{0,2,1:T(8,128)(2,1)S(1)} %maximum_convert_fusion.3) | copy-start | bytes 430084
  308.3 27.1 %copy-start.190 = (f32[224]{0:T(256)S(1)}, f32[224]{0:T(256)}, u32[]{:S(2)}) copy-start(f32[224]{0:T(256)} %copy-done.189) | copy-start | bytes 2692
  308.3 27.1 %copy-start.192 = (f32[224]{0:T(256)S(1)}, f32[224]{0:T(256)}, u32[]{:S(2)}) copy-start(f32[224]{0:T(256)} %copy-done.191) | copy-start | bytes 2692
  308.3 27.1 %copy-start.207 = (f32[224]{0:T(256)S(1)}, f32[224]{0:T(256)}, u32[]{:S(2)}) copy-start(f32[224]{0:T(256)} %get-tuple-element.151) | copy-start | bytes 2692
  338.1 3.8 collective-permute-start.2
  376.7 55.0 %reduce-scatter.46.cloned.1.call-start = ((), (), s32[]{:S(2)}) async-start(), calls=%async_computation.20 | async-start | bytes 860160
  389.1 115.3 %reduce-scatter.50.cloned.1.call-start = ((), (), s32[]{:S(2)}) async-start(), calls=%async_computation.22 | async-start | bytes 860160
  409.2 25.6 %copy-start.188 = (f32[224]{0:T(256)S(1)}, f32[224]{0:T(256)}, u32[]{:S(2)}) copy-start(f32[224]{0:T(256)} %get-tuple-element.148) | copy-start | bytes 2692
  409.2 25.6 %copy-start.194 = (f32[224]{0:T(256)S(1)}, f32[224]{0:T(256)}, u32[]{:S(2)}) copy-start(f32[224]{0:T(256)} %get-tuple-element.147) | copy-start | bytes 2692
  436.2 3.7 collective-permute-start.3
  478.7 54.3 %reduce-scatter.48.cloned.1.call-start = ((), (), s32[]{:S(2)}) async-start(), calls=%async_computation.21 | async-start | bytes 860160
  492.3 126.1 %reduce-scatter.54.cloned.1.call-start = ((), (), s32[]{:S(2)}) async-start(), calls=%async_computation.24 | async-start | bytes 921600
  507.5 112.5 %reduce-scatter.52.cloned.1.call-start = ((), (), s32[]{:S(2)}) async-start(), calls=%async_computation.23 | async-start | bytes 921600
  514.6 19.5 %copy-start.147 = (f32[224,32]{0,1:T(8,128)S(1)}, f32[224,32]{0,1:T(8,128)}, u32[]{:S(2)}) copy-start(f32[224,32]{0,1:T(8,128)} %get-tuple-element.125) | copy-start | bytes 86020
  514.6 20.4 %copy-start.7 = (bf16[3,224,960]{2,1,0:T(8,128)(2,1)S(1)}, bf16[3,224,960]{2,1,0:T(8,128)(2,1)}, u32[]{:S(2)}) copy-start(bf16[3,224,960]{2,1,0:T(8,128)(2,1)} %copy-done.5) | copy-start | bytes 3870724
  539.7 138.1 %reduce-scatter.56.cloned.1.call-start = ((), (), s32[]{:S(2)}) async-start(), calls=%async_computation.25 | async-start | bytes 6553600
  559.4 163.1 %reduce-scatter.34.cloned.1.call-start = ((), (), s32[]{:S(2)}) async-start(), calls=%async_computation.14 | async-start | bytes 2457600 | tf_op jit(solution)/shard_map/reduce_scatter | solution.py:391
  565.6 200.5 %reduce-scatter.32.cloned.1.call-start = ((), (), s32[]{:S(2)}) async-start(), calls=%async_computation.13 | async-start | bytes 2457600 | tf_op jit(solution)/shard_map/reduce_scatter | solution.py:391
  575.0 280.9 %reduce-scatter.38.cloned.1.call-start = ((), (), s32[]{:S(2)}) async-start(), calls=%async_computation.16 | async-start | bytes 6144000 | tf_op jit(solution)/shard_map/reduce_scatter | solution.py:391
  593.7 353.7 %reduce-scatter.36.cloned.1.call-start = ((), (), s32[]{:S(2)}) async-start(), calls=%async_computation.15 | async-start | bytes 6144000 | tf_op jit(solution)/shard_map/reduce_scatter | solution.py:391
  609.8 435.2 %all-reduce.7.cloned.1.call-start = ((), (), s32[]{:S(2)}) async-start(), calls=%async_computation.26 | async-start | bytes 9994240 | tf_op jit(solution)/shard_map/psum | solution.py:394
  (221 other events, 815.7 us)
Sparse Core Ops, SparseCore 0:
  277.7 25.8 reduce-scatter.39
  306.7 25.5 reduce-scatter.41
  376.8 25.6 reduce-scatter.43
  406.1 25.6 reduce-scatter.45
  478.8 25.5 reduce-scatter.49
  507.4 25.5 reduce-scatter.47
  535.3 22.8 reduce-scatter.53
  560.5 22.0 reduce-scatter.51
  584.9 92.8 reduce-scatter.55
  680.5 41.9 reduce-scatter.33
  725.4 40.6 reduce-scatter.31
  768.3 87.6 reduce-scatter.37
  858.4 88.9 reduce-scatter.35
  952.1 92.7 all-reduce.6
where the time goes:
time: 1070 us; the launch traced here: 1060 us
  waiting for transfers between devices  478 us (45%)
  matrix products  257 us (24%)
  local copies, waits for them, and re-layouts  121 us (11%)
  blocking collectives  91.3 us (9%)
  other arithmetic  90.4 us (8%)
  between operations  18 us (2%)
    reduce_scatter x4, waiting for transfers between devices, shards(): lax.psum_scatter(as_sent(summed), 'dp', scatter_dimension=0, tiled=True)  267 us
    unnamed x23, waiting for transfers between devices  147 us
    unnamed x493, local copies, waits for them, and re-layouts  69.8 us
    dot_general x21, matrix products, outer_sum(): lax.dot_general(left, right, (((0,), (0,)), ((), ())), preferred_element_...  64.3 us
    psum x1, waiting for transfers between devices, shards(): lax.psum(as_sent(summed), ('section', 'ctx'))  61.1 us
    dot_general x21, matrix products, product_back(): lax.dot_general(left, right, (((1,), (1,)), ((), ())), preferred_element_...  60.4 us
    dot_general x21, matrix products, weighted_product(): return jnp.dot(left, right, preferred_element_type=jnp.float32)  38.4 us
    all_gather x3, blocking collectives, forward_layer(): lax.all_gather(key_local, 'ctx', axis=0, tiled=True)  32.9 us
  transfers between devices with their start and end apart: 18, of which 14 were waited for; matrix products, arithmetic and copies ran while one was open for 17% of the time, Pallas kernels for 0%

commit v1 on v0

v1 whole, which is shorter than its diff:
```python
import functools

import jax
import jax.numpy as jnp
from jax import lax
from jax.experimental import pallas as pl
from jax.experimental.pallas import tpu as pltpu
from jax.sharding import PartitionSpec as P

MESH = pl.DeviceIdType.MESH
QUERY_HEADS = 15
KEY_VALUE_HEADS = 5
HEAD_SIZE = 64
SHARE = QUERY_HEADS // KEY_VALUE_HEADS
RANKS = 4
epsilon = 1e-05
masked_fill = -1e30
F32 = jnp.float32
BF16 = jnp.bfloat16


def dot(left, right):
    return jnp.dot(left, right, preferred_element_type=F32)


def dot_rt(left, right):
    return lax.dot_general(left, right, (((1,), (1,)), ((), ())), preferred_element_type=F32)


def dot_lt(left, right):
    return lax.dot_general(left, right, (((0,), (0,)), ((), ())), preferred_element_type=F32)


def tiles(total, width):
    return [(at, min(width, total - at)) for at in range(0, total, width)]


def wide(block):
    missing = 128 - block.shape[1]
    if not missing:
        return block
    return jnp.concatenate([block, jnp.zeros((block.shape[0], missing), block.dtype)], axis=1)


def lanes(rows):
    return lax.broadcasted_iota(jnp.int32, (rows, 128), 1)


def half_turn(block):
    front = lanes(block.shape[0]) % HEAD_SIZE < HEAD_SIZE // 2
    return jnp.where(front, pltpu.roll(block, 96, 1), pltpu.roll(block, 32, 1))


def inverse_rms(hidden):
    return lax.rsqrt(jnp.mean(hidden * hidden, axis=-1, keepdims=True) + epsilon)


def layers_kernel(
    ends, cosines, sines, seg_keys, seg_mine, gains, wq_h, wkv_h, wo_h, wg_h, wu_h, wd_h,
    acts_o, grads_o, gain_o, nf_o, in_o, gg_o, gu_o, br_o, la_o, ra_o, nr_o, kvg_o,
    wq, wkv, wo, wg, wu, wd,
    act, go, middle, norm_ffn, fact_a, fact_b, inner, lm, qd, kv, o_raw,
    sum_acc, gm, gg, gu, br, ra, dq_raw, pds, dkv, dkv_in, gkv,
    w_sem, in_send, in_recv, kv_send, kv_recv, dk_send, dk_recv, out_send, out_recv,
    op_own, op_send, op_recv,
):
    section = lax.axis_index("section")
    dp = lax.axis_index("dp")
    ctx = lax.axis_index("ctx")
    micro = ctx // 2
    xbit = ctx % 2
    rank = 2 * section + xbit
    rows, width = act.shape[1], act.shape[2]
    ff = wg.shape[1]
    ff_half = ff // 2

    def device_of(r):
        return (r // 2, dp, 2 * micro + r % 2)

    partner = (1 - section, dp, ctx)

    loads = [
        pltpu.make_async_copy(h, v, w_sem.at[i])
        for i, (h, v) in enumerate(
            [(wkv_h, wkv), (wq_h, wq), (wo_h, wo), (wg_h, wg), (wu_h, wu), (wd_h, wd)]
        )
    ]
    kv[...] = jnp.zeros_like(kv)
    barrier = pltpu.get_barrier_semaphore()
    for step in range(1, 8):
        other = (4 * section + ctx + step) % 8
        pl.semaphore_signal(
            barrier, inc=1, device_id=(other // 4, dp, other % 4), device_id_type=MESH
        )
    pl.semaphore_wait(barrier, 7)

    def in_copy(block, into_x):
        dst = act.at[0] if into_x else go.at[2]
        slot = 0 if into_x else 1
        return (
            pltpu.make_async_copy(ends.at[0, block], dst, in_recv.at[slot]),
            pltpu.make_async_remote_copy(
                src_ref=ends.at[0, block],
                dst_ref=dst,
                send_sem=in_send.at[block],
                recv_sem=in_recv.at[slot],
                device_id=(ctx // 2, dp, 2 * block + xbit),
                device_id_type=MESH,
            ),
        )

    def in_mine(block):
        return (section == ctx // 2) & (ctx // 2 == block)

    for block in range(2):
        for into_x in (True, False):
            here = section == (0 if into_x else 1)
            local, remote = in_copy(block, into_x)

            @pl.when(here & in_mine(block))
            def _(local=local):
                local.start()

            @pl.when(here & jnp.logical_not(in_mine(block)))
            def _(remote=remote):
                remote.start()

    for load in loads:
        load.start()

    lane = lanes(rows)
    low = lane < HEAD_SIZE
    cos_q = cosines[...]
    sin_q = sines[...]
    gain_attn = gains[0:1, :]
    gain_ffn = gains[1:2, :]

    def mask():
        query_index = rank * rows + lax.broadcasted_iota(jnp.int32, (rows, RANKS * rows), 0)
        key_index = lax.broadcasted_iota(jnp.int32, (rows, RANKS * rows), 1)
        ok = (seg_mine[:, 0:1] == seg_keys[0:1, :]) & (query_index >= key_index)
        return jnp.where(ok, 0.0, masked_fill)

    def kv_rows(l, r):
        return kv.at[l, pl.ds(pl.multiple_of(r * rows, 16), rows)]

    def kv_copy(l, quarter, dst, slot):
        return pltpu.make_async_remote_copy(
            src_ref=kv_rows(l, quarter),
            dst_ref=kv_rows(l, quarter),
            send_sem=kv_send.at[l, slot],
            recv_sem=kv_recv.at[l, quarter],
            device_id=device_of(dst),
            device_id_type=MESH,
        )

    kv_plan = [(0, 0, 1, 0), (0, 0, 2, 1), (1, 1, 2, 0), (1, 1, 3, 1), (2, 2, 3, 0)]
    kv_relay = (1, 0, 3, 2)

    def kv_start(l):
        for sender, quarter, dst, slot in kv_plan:

            @pl.when(rank == sender)
            def _(quarter=quarter, dst=dst, slot=slot):
                kv_copy(l, quarter, dst, slot).start()

    def kv_finish(l):
        @pl.when(rank == 1)
        def _():
            kv_copy(l, 0, 3, 2).wait_recv()
            kv_copy(l, 0, 3, 2).start()

        for quarter, receivers in ((0, (2, 3)), (1, (2, 3)), (2, (3,))):
            for receiver in receivers:

                @pl.when(rank == receiver)
                def _(quarter=quarter):
                    kv_copy(l, quarter, 0, 0).wait_recv()

    def kv_sent(l):
        for sender, quarter, dst, slot in kv_plan + [kv_relay]:

            @pl.when(rank == sender)
            def _(quarter=quarter, dst=dst, slot=slot):
                kv_copy(l, quarter, dst, slot).wait_send()

    def out_copy(array, out, l, kind):
        home = 2 * section + xbit
        return (
            pltpu.make_async_copy(array, out.at[0, micro], out_recv.at[kind, micro]),
            pltpu.make_async_remote_copy(
                src_ref=array,
                dst_ref=out.at[0, micro],
                send_sem=out_send.at[kind, l],
                recv_sem=out_recv.at[kind, micro],
                device_id=(l, dp, home),
                device_id_type=MESH,
            ),
        )

    def out_mine(l):
        return (section == l) & (ctx == 2 * section + xbit)

    def out_start(array, out, l, kind):
        local, remote = out_copy(array, out, l, kind)

        @pl.when(out_mine(l))
        def _():
            local.start()

        @pl.when(jnp.logical_not(out_mine(l)))
        def _():
            remote.start()

    place = [pl.ds((2 * c + l) * rows, rows) for c in range(2) for l in range(2)]

    def op_rows(l):
        return pl.ds(pl.multiple_of((2 * section + l) * rows, 16), rows)

    def op_copy(kind, l, own):
        role = section if own else 1 - section
        half = pl.ds(pl.multiple_of(role * ff_half, 128), ff_half)
        src = [
            lambda: norm_ffn.at[l],
            lambda: inner.at[l],
            lambda: gg.at[:, half],
            lambda: gu.at[:, half],
            lambda: br.at[:, pl.ds(pl.multiple_of(role * 512, 128), 512)],
            lambda: lm.at[l, role],
            lambda: ra.at[role],
            lambda: lm.at[l, 0],
            lambda: gkv.at[:, pl.ds(pl.multiple_of(role * 256, 128), 384)],
        ][kind]()
        dst = [nf_o, in_o, gg_o, gu_o, br_o, la_o, ra_o, nr_o, kvg_o][kind].at[op_rows(l)]
        if own:
            return pltpu.make_async_copy(src, dst, op_own.at[kind, l])
        return pltpu.make_async_remote_copy(
            src_ref=src,
            dst_ref=dst,
            send_sem=op_send.at[kind, l],
            recv_sem=op_recv.at[kind, l],
            device_id=partner,
            device_id_type=MESH,
        )

    def op_start(kinds, l):
        for kind in kinds:
            op_copy(kind, l, True).start()
            op_copy(kind, l, False).start()

    def op_sent(kinds, l):
        for kind in kinds:
            op_copy(kind, l, True).wait()
            op_copy(kind, l, False).wait_send()

    @pl.when(section == 0)
    def _():
        for block in range(2):

            @pl.when(jnp.logical_not(in_mine(block)))
            def _(block=block):
                in_copy(block, True)[1].wait_send()

    @pl.when(section == 1)
    def _():
        for block in range(2):

            @pl.when(jnp.logical_not(in_mine(block)))
            def _(block=block):
                in_copy(block, False)[1].wait_send()

    in_copy(0, True)[1].wait_recv()
    loads[0].wait()

    def forward(l, carry):
        hidden = act[l].astype(F32)
        lm[l, 0] = (hidden * inverse_rms(hidden) * gain_attn).astype(BF16)
        cos_kv = jnp.where(low, cos_q, 1.0)
        sin_kv = jnp.where(low, sin_q, 0.0)
        mine = pl.ds(pl.multiple_of(rank * rows, 16), rows)
        for g in range(KEY_VALUE_HEADS):
            block = dot(lm[l, 0], wkv[:, 128 * g : 128 * g + 128])
            turned = block * cos_kv + half_turn(block) * sin_kv
            kv[l, mine, 128 * g : 128 * g + 128] = turned.astype(BF16)
        kv_start(l)

        @pl.when(l == 0)
        def _():
            loads[1].wait()

        for at, size in tiles(width, 256):
            product = dot(lm[l, 0], wq[:, at : at + size])
            for inside, part in tiles(size, 128):
                block = wide(product[:, inside : inside + part])
                turned = (block * cos_q + half_turn(block) * sin_q) * 0.125
                head = (at + inside) // HEAD_SIZE
                qd[l, head // SHARE, pl.ds(head % SHARE * rows, rows), :] = jnp.where(
                    low, turned, 0.0
                ).astype(BF16)
                head += 1
                if head < QUERY_HEADS:
                    qd[l, head // SHARE, pl.ds(head % SHARE * rows, rows), :] = jnp.where(
                        low, pltpu.roll(turned, 64, 1), 0.0
                    ).astype(BF16)
        kv_finish(l)
        allowed = mask()

        def heads(g, carry):
            kv_g = kv[l, :, pl.ds(pl.multiple_of(g * 128, 128), 128)]
            for i in range(SHARE):
                scores = dot_rt(qd[l, g, i * rows : (i + 1) * rows, :], kv_g) + allowed
                peak = jnp.max(scores, axis=-1, keepdims=True)
                exponent = jnp.exp(scores - peak)
                total = jnp.sum(exponent, axis=-1, keepdims=True)
                out = dot(exponent.astype(BF16), kv_g) / total
                o_raw[l, g * SHARE + i] = jnp.where(low, peak + jnp.log(total), out)
            return carry

        lax.fori_loop(0, KEY_VALUE_HEADS, heads, 0)
        for at, size in tiles(width, 128):
            head = at // HEAD_SIZE
            block = pltpu.roll(o_raw[l, head], 64, 1)
            if size == 128:
                block = jnp.where(low, block, o_raw[l, head + 1])
            lm[l, 1, :, at : at + size] = block[:, :size].astype(BF16)

        @pl.when(l == 0)
        def _():
            loads[2].wait()

        for at, size in tiles(width, 256):
            middle[l, :, at : at + size] = act[l, :, at : at + size].astype(F32) + dot(
                lm[l, 1], wo[:, at : at + size]
            )
        mid = middle[l]
        norm_ffn[l] = (mid * inverse_rms(mid) * gain_ffn).astype(BF16)

        @pl.when(l == 0)
        def _():
            loads[3].wait()
            loads[4].wait()

        def gates(j, carry):
            part = pl.ds(pl.multiple_of(j * 256, 256), 256)
            gate = dot(norm_ffn[l], wg[:, part])
            upper = dot(norm_ffn[l], wu[:, part])
            s = jax.nn.sigmoid(gate)
            swish = gate * s
            inner[l, :, part] = (swish * upper).astype(BF16)
            fact_a[l, :, part] = (upper * s * (1.0 + gate * (1.0 - s))).astype(BF16)
            fact_b[l, :, part] = swish.astype(BF16)
            return carry

        lax.fori_loop(0, ff // 256, gates, 0)

        @pl.when(l == 0)
        def _():
            loads[5].wait()

        for at, size in tiles(width, 256):
            act[l + 1, :, at : at + size] = (
                middle[l, :, at : at + size] + dot(inner[l], wd[:, at : at + size])
            ).astype(BF16)
        out_start(act.at[l + 1], acts_o, l, 0)
        op_start((0, 1, 7), l)
        kv_sent(l)
        return carry

    lax.fori_loop(0, 2, forward, 0)

    in_copy(0, False)[1].wait_recv()
    gain_o[...] = jnp.zeros_like(gain_o)
    br[...] = jnp.zeros_like(br)

    def dk_copy(l, src_quarter, count, dst, slot_in, slot):
        return pltpu.make_async_remote_copy(
            src_ref=dkv.at[pl.ds(src_quarter * rows, count * rows)],
            dst_ref=dkv_in.at[l, pl.ds(slot_in * rows, count * rows)],
            send_sem=dk_send.at[l, slot],
            recv_sem=dk_recv.at[l, slot_in],
            device_id=device_of(dst),
            device_id_type=MESH,
        )

    def backward(step, carry):
        l = 1 - step

        @pl.when(l == 0)
        def _():
            op_sent((2, 3, 4, 5, 6, 8), 1)

        branch = go[l + 1]
        br[:, :width] = branch
        op_start((4,), l)

        def gates(j, carry):
            part = pl.ds(pl.multiple_of(j * 256, 256), 256)
            grad_inner = dot_rt(go[l + 1], wd[part, :])
            gg[:, part] = (grad_inner * fact_a[l, :, part].astype(F32)).astype(BF16)
            gu[:, part] = (grad_inner * fact_b[l, :, part].astype(F32)).astype(BF16)
            return carry

        lax.fori_loop(0, ff // 256, gates, 0)
        op_start((2, 3), l)
        for at, size in tiles(width, 256):
            sum_acc[:, at : at + size] = dot_rt(gg[...], wg[at : at + size, :]) + dot_rt(
                gu[...], wu[at : at + size, :]
            )

        def norm_back(hidden, gain, row):
            upstream = sum_acc[...]
            scale = inverse_rms(hidden)
            weighted = upstream * gain
            inside = jnp.mean(weighted * hidden, axis=-1, keepdims=True)
            gain_o[row : row + 1, :] += jnp.sum(upstream * hidden * scale, axis=0, keepdims=True)
            return scale * weighted - hidden * (scale * scale * scale * inside)

        gm[...] = go[l + 1].astype(F32) + norm_back(middle[l], gain_ffn, 1)
        ra[1] = gm[...].astype(BF16)

        for at, size in tiles(width, 256):
            product = dot_rt(ra[1], wo[at : at + size, :])
            for inside, part in tiles(size, 128):
                block = wide(product[:, inside : inside + part])
                head = (at + inside) // HEAD_SIZE
                qd[l, head // SHARE, pl.ds((SHARE + head % SHARE) * rows, rows), :] = jnp.where(
                    low, 0.0, pltpu.roll(block, 64, 1)
                ).astype(BF16)
                head += 1
                if head < QUERY_HEADS:
                    qd[l, head // SHARE, pl.ds((SHARE + head % SHARE) * rows, rows), :] = (
                        jnp.where(low, 0.0, block).astype(BF16)
                    )
        allowed = mask()

        def heads(g, carry):
            kv_g = kv[l, :, pl.ds(pl.multiple_of(g * 128, 128), 128)]
            for i in range(SHARE):
                mine = slice(i * rows, (i + 1) * rows)
                other = slice((SHARE + i) * rows, (SHARE + i + 1) * rows)
                kept = o_raw[l, g * SHARE + i]
                log_total = kept[:, 0:1]
                scores = dot_rt(qd[l, g, mine, :], kv_g) + allowed
                probs = jnp.exp(scores - log_total)
                grad_out = qd[l, g, other, :]
                grad_probs = dot_rt(grad_out, kv_g)
                weight = jnp.sum(grad_out.astype(F32) * kept, axis=-1, keepdims=True)
                grad_scores = (probs * (grad_probs - weight)).astype(BF16)
                pds[mine, :] = grad_scores
                pds[other, :] = probs.astype(BF16)
                dq_raw[g * SHARE + i] = dot(grad_scores, kv_g)
            grad_kv = dot_lt(qd[l, g], pds[...])
            dkv[:, pl.ds(pl.multiple_of(g * 128, 128), 128)] = grad_kv.T.astype(BF16)
            return carry

        lax.fori_loop(0, KEY_VALUE_HEADS, heads, 0)

        @pl.when(rank == 3)
        def _():
            dk_copy(l, 2, 1, 2, 0, 0).start()
            dk_copy(l, 0, 2, 1, 0, 1).start()

        @pl.when(rank == 2)
        def _():
            dk_copy(l, 1, 1, 1, 2, 0).start()
            dk_copy(l, 0, 1, 0, 1, 1).start()

        @pl.when(rank == 1)
        def _():
            dk_copy(l, 0, 2, 1, 0, 0).wait_recv()
            dkv[:rows] = (dkv[:rows].astype(F32) + dkv_in[l, :rows].astype(F32)).astype(BF16)
            dk_copy(l, 0, 1, 0, 0, 0).start()

        for at, size in tiles(width, 128):
            head = at // HEAD_SIZE
            block = dq_raw[head]
            if size == 128:
                block = jnp.where(low, block, pltpu.roll(dq_raw[head + 1], 64, 1))
            turned = (block * cos_q - half_turn(block) * sin_q) * 0.125
            ra[0, :, at : at + size] = turned[:, :size].astype(BF16)
        op_start((5, 6), l)

        @pl.when(rank == 3)
        def _():
            dk_copy(l, 2, 1, 2, 0, 0).wait_send()
            dk_copy(l, 0, 2, 1, 0, 1).wait_send()

        @pl.when(rank == 2)
        def _():
            dk_copy(l, 0, 1, 2, 0, 0).wait_recv()
            dk_copy(l, 1, 1, 1, 2, 0).wait_send()
            dk_copy(l, 0, 1, 0, 1, 1).wait_send()
            dkv[2 * rows : 3 * rows] = (
                dkv[2 * rows : 3 * rows].astype(F32) + dkv_in[l, :rows].astype(F32)
            ).astype(BF16)

        @pl.when(rank == 1)
        def _():
            dk_copy(l, 0, 1, 2, 2, 0).wait_recv()
            dk_copy(l, 0, 1, 0, 0, 0).wait_send()
            dkv[rows : 2 * rows] = (
                dkv[rows : 2 * rows].astype(F32)
                + dkv_in[l, rows : 2 * rows].astype(F32)
                + dkv_in[l, 2 * rows :].astype(F32)
            ).astype(BF16)

        @pl.when(rank == 0)
        def _():
            dk_copy(l, 0, 1, 2, 0, 0).wait_recv()
            dk_copy(l, 0, 1, 2, 1, 0).wait_recv()
            dkv[:rows] = (
                dkv[:rows].astype(F32)
                + dkv_in[l, :rows].astype(F32)
                + dkv_in[l, rows : 2 * rows].astype(F32)
            ).astype(BF16)

        cos_kv = jnp.where(low, cos_q, 1.0)
        sin_kv = jnp.where(low, sin_q, 0.0)
        mine = pl.ds(pl.multiple_of(rank * rows, 16), rows)
        for g in range(KEY_VALUE_HEADS):
            part = slice(128 * g, 128 * g + 128)
            block = dkv[mine, part].astype(F32)
            gkv[:, part] = (block * cos_kv - half_turn(block) * sin_kv).astype(BF16)
        op_start((8,), l)
        for at, size in tiles(width, 256):
            sum_acc[:, at : at + size] = dot_rt(ra[0], wq[at : at + size, :]) + dot_rt(
                gkv[...], wkv[at : at + size, :]
            )
        go[l] = (gm[...] + norm_back(act[l].astype(F32), gain_attn, 0)).astype(BF16)
        out_start(go.at[l], grads_o, l, 1)
        return carry

    lax.fori_loop(0, 2, backward, 0)

    op_sent((2, 3, 4, 5, 6, 8), 0)
    for l in range(2):
        op_sent((0, 1, 7), l)
        for kind in range(9):
            op_copy(kind, l, False).wait_recv()
        for kind, out, array in ((0, acts_o, act.at[l + 1]), (1, grads_o, go.at[l])):

            @pl.when(jnp.logical_not(out_mine(l)))
            def _(l=l, kind=kind, out=out, array=array):
                out_copy(array, out, l, kind)[1].wait_send()

    for kind, out in ((0, acts_o), (1, grads_o)):
        for block in range(2):
            pltpu.make_async_copy(act.at[0], out.at[0, block], out_recv.at[kind, block]).wait()


def run_layers(ends, cosines, sines, seg_keys, seg_mine, gains, weights):
    micro_count, rows, width = ends.shape[1:]
    wq, wkv, wo, wg, wu, wd = weights
    ff = wg.shape[1]
    keys = RANKS * rows
    kv_width = wkv.shape[1]
    vmem, hbm = pl.BlockSpec(memory_space=pltpu.VMEM), pl.BlockSpec(memory_space=pl.ANY)
    op_rows = 4 * rows
    out = lambda *shape: jax.ShapeDtypeStruct(shape, BF16)
    dma = pltpu.SemaphoreType.DMA
    return pl.pallas_call(
        layers_kernel,
        out_shape=[
            out(*ends.shape),
            out(*ends.shape),
            jax.ShapeDtypeStruct((8, width), F32),
            out(op_rows, width),
            out(op_rows, ff),
            out(op_rows, ff // 2),
            out(op_rows, ff // 2),
            out(op_rows, 512),
            out(op_rows, width),
            out(op_rows, width),
            out(op_rows, width),
            out(op_rows, 384),
        ],
        in_specs=[hbm] + [vmem] * 5 + [hbm] * 6,
        out_specs=[hbm, hbm, vmem] + [hbm] * 9,
        scratch_shapes=[
            pltpu.VMEM(wq.shape, BF16),
            pltpu.VMEM(wkv.shape, BF16),
            pltpu.VMEM(wo.shape, BF16),
            pltpu.VMEM(wg.shape, BF16),
            pltpu.VMEM(wu.shape, BF16),
            pltpu.VMEM(wd.shape, BF16),
            pltpu.VMEM((3, rows, width), BF16),
            pltpu.VMEM((3, rows, width), BF16),
            pltpu.VMEM((2, rows, width), F32),
            pltpu.VMEM((2, rows, width), BF16),
            pltpu.VMEM((2, rows, ff), BF16),
            pltpu.VMEM((2, rows, ff), BF16),
            pltpu.VMEM((2, rows, ff), BF16),
            pltpu.VMEM((2, 2, rows, width), BF16),
            pltpu.VMEM((2, KEY_VALUE_HEADS, 2 * SHARE * rows, 128), BF16),
            pltpu.VMEM((2, keys, kv_width), BF16),
            pltpu.VMEM((2, QUERY_HEADS, rows, 128), F32),
            pltpu.VMEM((rows, width), F32),
            pltpu.VMEM((rows, width), F32),
            pltpu.VMEM((rows, ff), BF16),
            pltpu.VMEM((rows, ff), BF16),
            pltpu.VMEM((rows, 1024), BF16),
            pltpu.VMEM((2, rows, width), BF16),
            pltpu.VMEM((QUERY_HEADS, rows, 128), F32),
            pltpu.VMEM((2 * SHARE * rows, keys), BF16),
            pltpu.VMEM((keys, kv_width), BF16),
            pltpu.VMEM((2, 3 * rows, kv_width), BF16),
            pltpu.VMEM((rows, kv_width), BF16),
            dma((6,)),
            dma((2,)),
            dma((2,)),
            dma((2, 3)),
            dma((2, 3)),
            dma((2, 2)),
            dma((2, 3)),
            dma((2, 2)),
            dma((2, 2)),
            dma((9, 2)),
            dma((9, 2)),
            dma((9, 2)),
        ],
        compiler_params=pltpu.CompilerParams(
            collective_id=1, has_side_effects=True, vmem_limit_bytes=61 * 2**20
        ),
        name="layers",
    )(ends, cosines, sines, seg_keys, seg_mine, gains, wq, wkv, wo, wg, wu, wd)


def shards(
    ends,
    doc_lengths,
    w_query,
    key_projection_weight,
    value_projection_weight,
    w_out,
    w_gate,
    w_up,
    w_down,
    gain_attn,
    gain_ffn,
):
    rows, width = ends.shape[2:]
    section = lax.axis_index("section")
    ctx = lax.axis_index("ctx")
    row_tokens = rows * lax.axis_size("ctx")
    rank = 2 * section + ctx % 2
    lengths = lax.dynamic_index_in_dim(doc_lengths, ctx // 2, 0, keepdims=False)[0]

    def place(token_index):
        segment = jnp.zeros_like(token_index)
        start = jnp.zeros_like(token_index)
        finish = jnp.int32(0)
        for slot in range(lengths.shape[0]):
            finish = finish + lengths[slot]
            passed = (token_index >= finish).astype(jnp.int32)
            segment = segment + passed
            start = start + passed * lengths[slot]
        return segment, token_index - start

    seg_keys, _ = place(lax.broadcasted_iota(jnp.int32, (8, row_tokens), 1))
    seg_mine, token_position = place(
        rank * rows + lax.broadcasted_iota(jnp.int32, (rows, 128), 0)
    )
    lane = lax.broadcasted_iota(jnp.int32, (rows, 128), 1)
    half = HEAD_SIZE // 2
    frequency = 10000.0 ** (-2.0 * (lane % half).astype(F32) / HEAD_SIZE)
    angles = token_position.astype(F32) * frequency
    cosines = jnp.cos(angles)
    sines = jnp.where(lane % HEAD_SIZE < half, -1.0, 1.0) * jnp.sin(angles)
    w_kv = jnp.stack(
        [
            key_projection_weight.reshape(width, KEY_VALUE_HEADS, HEAD_SIZE),
            value_projection_weight.reshape(width, KEY_VALUE_HEADS, HEAD_SIZE),
        ],
        axis=2,
    ).reshape(width, 2 * KEY_VALUE_HEADS * HEAD_SIZE)
    gains = jnp.concatenate(
        [jnp.stack([gain_attn, gain_ffn]).astype(F32), jnp.zeros((6, width), F32)]
    )
    acts, grads_in, gain_sums, nf, inner, gg, gu, br, la, ra, nr, kvg = run_layers(
        ends,
        cosines,
        sines,
        seg_keys,
        seg_mine,
        gains,
        (w_query, w_kv, w_out, w_gate, w_up, w_down),
    )

    def reduced(left, right):
        total = lax.dot_general(
            left, right, (((0,), (0,)), ((), ())), preferred_element_type=F32
        ).astype(BF16)
        piece = lax.psum_scatter(total, "dp", scatter_dimension=0, tiled=True)
        return lax.psum(piece, "ctx")

    def both(piece, axis):
        return lax.all_gather(piece, "section", axis=axis, tiled=axis > 0).astype(F32)

    grad_gate = both(reduced(nf, gg), 1)
    grad_up = both(reduced(nf, gu), 1)
    grad_down = both(reduced(inner, br), 1)[:, :width]
    attn = both(reduced(la, ra), 0)
    kv_parts = both(reduced(nr, kvg), 0)
    kv_grad = jnp.concatenate([kv_parts[0], kv_parts[1][:, 128:]], axis=1).reshape(
        -1, KEY_VALUE_HEADS, 2, HEAD_SIZE
    )
    grad_key = kv_grad[:, :, 0].reshape(kv_grad.shape[0], -1)
    grad_value = kv_grad[:, :, 1].reshape(kv_grad.shape[0], -1)
    gain_sum = lax.psum(gain_sums[:2], ("section", "ctx"))
    gain_piece = lax.psum_scatter(gain_sum, "dp", scatter_dimension=1, tiled=True)
    return (
        acts,
        grads_in,
        attn[0],
        grad_key,
        grad_value,
        attn[1],
        grad_gate,
        grad_up,
        grad_down,
        gain_piece[0],
        gain_piece[1],
    )


def solution(mesh):
    return jax.shard_map(
        shards,
        mesh=mesh,
        in_specs=(P("section", None, ("dp", "ctx"), None), P(None, "dp", None)) + (P(),) * 9,
        out_specs=(P("section", None, ("dp", "ctx"), None),) * 2
        + (P("dp", None),) * 7
        + (P("dp"),) * 2,
        check_vma=False,
    )
```

time: 1070 us -> 525 us (0.49)
  matrix products: 257 us -> 27.5 us
  waiting for transfers between devices: 478 us -> 303 us
  Pallas kernels: 0 us -> 117 us
  local copies, waits for them, and re-layouts: 121 us -> 26.5 us
  other arithmetic: 90.4 us -> 13.1 us
  blocking collectives: 91.3 us -> 19.5 us
    dot_general x144 -> x5, matrix products: 257 us -> 27.5 us  [reduced(): lax.dot_general(left, right, (((0,), (0,)), ((), ())), preferred_element_...]
    unnamed x23 -> x11, waiting for transfers between devices: 147 us -> 24.4 us
    pallas_call x0 -> x1, Pallas kernels: none -> 117 us  [run_layers(): pl.pallas_call(layers_kernel, out_shape=[out(*ends.shape), out(*ends.shap...]
    reduce_scatter x4 -> x5, waiting for transfers between devices: 267 us -> 196 us  [reduced(): piece = lax.psum_scatter(total, 'dp', scatter_dimension=0, tiled=True)]
    all_gather x6 -> x2, blocking collectives: 64.6 us -> 5.01 us  [both(): lax.all_gather(piece, 'section', axis=axis, tiled=axis > 0).astype(F32)]
    unnamed x493 -> x24, local copies, waits for them, and re-layouts: 69.8 us -> 17.8 us
    convert_element_type x38 -> x4, other arithmetic: 29.7 us -> 6.3 us  [both(): lax.all_gather(piece, 'section', axis=axis, tiled=axis > 0).astype(F32)]
    another operation x27 -> x1, other arithmetic: 24.8 us -> 1.41 us  [shards(): jnp.stack([key_projection_weight.reshape(width, KEY_VALUE_HEADS, HEAD_SIZ...]
  transfers between devices with their start and end apart: 18 -> 10, of which waited for: 14 -> 7; matrix products, arithmetic and copies ran while one was open for 17% -> 7% of each run, Pallas kernels for 0% -> 0%
where the time goes in v1:
time: 525 us; the launch traced here: 523 us
  waiting for transfers between devices  303 us (58%)
  Pallas kernels  117 us (22%)
  matrix products  27.5 us (5%)
  local copies, waits for them, and re-layouts  26.5 us (5%)
  blocking collectives  19.5 us (4%)
  between operations  15.7 us (3%)
  other arithmetic  13.1 us (2%)
    reduce_scatter x5, waiting for transfers between devices, reduced(): piece = lax.psum_scatter(total, 'dp', scatter_dimension=0, tiled=True)  196 us
    pallas_call x1, Pallas kernels, run_layers(): pl.pallas_call(layers_kernel, out_shape=[out(*ends.shape), out(*ends.shap...  117 us
    psum x1, waiting for transfers between devices, reduced(): return lax.psum(piece, 'ctx')  79.9 us
    dot_general x5, matrix products, reduced(): lax.dot_general(left, right, (((0,), (0,)), ((), ())), preferred_element_...  27.5 us
    unnamed x11, waiting for transfers between devices  24.4 us
    unnamed x24, local copies, waits for them, and re-layouts  17.8 us
    psum x1, blocking collectives, shards(): gain_sum = lax.psum(gain_sums[:2], ('section', 'ctx'))  14.4 us
  transfers between devices with their start and end apart: 10, of which 7 were waited for; matrix products, arithmetic and copies ran while one was open for 7% of the time, Pallas kernels for 0%

profile of v1, /device:TPU:0, one launch (start us, length us, event | category | flops | bytes accessed | tf_op | source)
XLA Modules:
  0.0 523.5 jit_solution(1871109195749940746)
XLA Ops:
  9.9 1.3 convert_add_fusion.1
  12.6 1.4 pad_maximum_fusion
  14.0 1.4 copy.36.wkv_h
  15.4 7.9 %copy.37.wd_h = bf16[2560,960]{1,0:T(8,128)(2,1)} copy(bf16[2560,960]{0,1:T(8,128)(2,1)} %param.19) | data formatting | bytes 9830400 | tf_op args[8]
  23.9 1.2 sine_multiply_fusion
  26.4 117.2 %layers.1 = (bf16[1,2,224,960]{3,2,1,0:T(8,128)(2,1)}, bf16[1,2,224,960]{3,2,1,0:T(8,128)(2,1)}, f32[8,960]{1,0:T(8,128)}, bf16[896,960]{1,0:T(8,128)(2,1)}, bf1...) custom-call(bf16[1,2,224,960]{3,2,1,0:T(8,128)(2,1)} %ends.1, ...), custom_call_target="tpu_custom_call" | custom-call | tf_op jit(solution)/shard_map/layers/pallas_call | solution.py:561
  143.6 3.7 convolution_convert_fusion.4
  147.4 5.7 %convolution_convert_fusion.3 = bf16[960,960]{1,0:T(8,128)(2,1)} fusion(bf16[896,960]{1,0:T(8,128)(2,1)} %get-tuple-element.25, bf16[896,960]{1,0:T(8,128)(2,1)} %get-tuple-element.26), kind=kOutput, calls=%fused_computation.3 | convolution fusion | flops 1652428800 | bytes 5283840 | tf_op jit(solution)/shard_map/dot_general | solution.py:690
  153.4 5.7 %convolution_convert_fusion.1 = bf16[960,1280]{1,0:T(8,128)(2,1)} fusion(bf16[896,960]{1,0:T(8,128)(2,1)} %get-tuple-element.29, bf16[896,1280]{1,0:T(8,128)(2,1)S(1)} %copy-done.7), kind=kOutput, calls=%fused_computation.1 | convolution fusion | flops 2203238400 | bytes 6471680 | tf_op jit(solution)/shard_map/dot_general | solution.py:690
  159.2 1.6 copy-done.6
  160.8 5.7 %convolution_convert_fusion.2 = bf16[960,1280]{1,0:T(8,128)(2,1)} fusion(bf16[896,960]{1,0:T(8,128)(2,1)} %get-tuple-element.29, bf16[896,1280]{1,0:T(8,128)(2,1)S(1)} %copy-done.6), kind=kOutput, calls=%fused_computation.2 | convolution fusion | flops 2203238400 | bytes 6471680 | tf_op jit(solution)/shard_map/dot_general | solution.py:690
  166.7 1.1 copy-done.8
  167.8 6.6 %convolution_convert_fusion = bf16[2560,512]{1,0:T(8,128)(2,1)} fusion(bf16[896,2560]{1,0:T(8,128)(2,1)} %get-tuple-element.32, bf16[896,512]{1,0:T(8,128)(2,1)S(1)} %copy-done.8), kind=kOutput, calls=%fused_computation | convolution fusion | flops 2350120960 | bytes 8126464 | tf_op jit(solution)/shard_map/dot_general | solution.py:690
  174.5 38.8 %reduce-scatter.9.cloned.1.call-done = bf16[240,960]{1,0:T(8,128)(2,1)} async-done(((bf16[960,960]{1,0:T(8,128)(2,1)}), bf16[240,960]{1,0:T(8,128)(2,1)}) %reduce-scatter.9.cloned.1.call-update) | async-done | bytes 460816 | tf_op jit(solution)/shard_map/reduce_scatter | solution.py:693
  213.3 51.7 %reduce-scatter.15.cloned.1.call-done = bf16[240,1280]{1,0:T(8,128)(2,1)} async-done(((bf16[960,1280]{1,0:T(8,128)(2,1)}), bf16[240,1280]{1,0:T(8,128)(2,1)}) %reduce-scatter.15.cloned.1.call-update) | async-done | bytes 614416 | tf_op jit(solution)/shard_map/reduce_scatter | solution.py:693
  265.0 51.9 %reduce-scatter.13.cloned.1.call-done = bf16[240,1280]{1,0:T(8,128)(2,1)} async-done(((bf16[960,1280]{1,0:T(8,128)(2,1)}), bf16[240,1280]{1,0:T(8,128)(2,1)}) %reduce-scatter.13.cloned.1.call-update) | async-done | bytes 614416 | tf_op jit(solution)/shard_map/reduce_scatter | solution.py:693
  316.9 53.8 %reduce-scatter.17.cloned.1.call-done = bf16[640,512]{1,0:T(8,128)(2,1)} async-done(((bf16[2560,512]{1,0:T(8,128)(2,1)}), bf16[640,512]{1,0:T(8,128)(2,1)}) %reduce-scatter.17.cloned.1.call-update) | async-done | bytes 655376 | tf_op jit(solution)/shard_map/reduce_scatter | solution.py:693
  371.6 1.0 copy.40
  372.7 79.9 %all-reduce.4.cloned.1.call-done = (bf16[1,240,960]{2,1,0:T(8,128)(2,1)}, bf16[1,240,384]{2,1,0:T(8,128)(2,1)}, bf16[240,1280]{1,0:T(8,128)(2,1)}, bf16[240,1280]{1,0:T(8,128)(2,1)}, bf16[640,512]{1,0:T(8,128)(2,1)}) async-done(((bf16[1,240,960]{2,1,0:T(8,128)(2,1)}, bf16[1,240,384]{2,1,0:T(8,128)(2,1)}, bf16[240,1280]{1,0:T(8,128)(2,1)}, bf16[240,1280]{1,0:T(8,128)(2,1)}, bf16[640,512]{1,0:T(8,128)(2,1)}), ...) | async-done | bytes 2529296 | tf_op jit(solution)/shard_map/psum | solution.py:694
  453.3 23.6 %reduce-scatter.19.cloned.1.call-done = f32[240,2]{1,0:T(8,128)} async-done(((f32[960,2]{1,0:T(8,128)}), f32[240,2]{1,0:T(8,128)}) %reduce-scatter.19.cloned.1.call-update) | async-done | bytes 1936
  476.9 1.0 copy.41
  477.8 14.4 %psum.48 = f32[2,240]{1,0:T(2,128)S(1)} all-reduce(f32[2,240]{1,0:T(2,128)S(1)} %copy.41), channel_id=1, replica_groups=mesh['section'=2,'dp'=4,'ctx'=4] {'section','ctx'}, use_global_device_ids=true, to_apply=%region_10.11 | all-reduce | flops 480 | bytes 3840 | tf_op jit(solution)/shard_map/psum | solution.py:709
  492.9 2.3 all_gather.24
  496.2 2.7 all_gather.22
  500.2 1.5 slice_bitcast_fusion
  501.7 3.0 convert_element_type.65
  504.7 3.0 convert_element_type.63
  507.7 2.8 all-gather.8.cloned.1.call-done
  510.5 1.6 slice_convert_fusion
  512.2 2.0 copy.39
  514.2 0.9 copy.49
  515.7 0.9 copy.50
  (59 shorter events, 10.2 us)
Async XLA Ops:
  7.2 0.1 copy-start
  7.2 167.3 %reduce-scatter.11.cloned.1.call-start = ((), (), s32[]{:S(2)}) async-start(), calls=%async_computation.7 | async-start | bytes 921600 | tf_op jit(solution)/shard_map/reduce_scatter | solution.py:693
  147.4 65.9 %reduce-scatter.9.cloned.1.call-start = ((), (), s32[]{:S(2)}) async-start(), calls=%async_computation.6 | async-start | bytes 2457600 | tf_op jit(solution)/shard_map/reduce_scatter | solution.py:693
  147.4 6.0 %copy-start.7 = (bf16[896,1280]{1,0:T(8,128)(2,1)S(1)}, bf16[896,1280]{1,0:T(8,128)(2,1)}, u32[]{:S(2)}) copy-start(bf16[896,1280]{1,0:T(8,128)(2,1)} %get-tuple-element.31) | copy-start | bytes 6881284
  153.2 111.8 %reduce-scatter.15.cloned.1.call-start = ((), (), s32[]{:S(2)}) async-start(), calls=%async_computation.10 | async-start | bytes 3072000 | tf_op jit(solution)/shard_map/reduce_scatter | solution.py:693
  159.2 1.7 copy-start.6
  159.2 157.7 %reduce-scatter.13.cloned.1.call-start = ((), (), s32[]{:S(2)}) async-start(), calls=%async_computation.8 | async-start | bytes 3072000 | tf_op jit(solution)/shard_map/reduce_scatter | solution.py:693
  166.6 1.2 copy-start.8
  166.6 204.1 %reduce-scatter.17.cloned.1.call-start = ((), (), s32[]{:S(2)}) async-start(), calls=%async_computation.12 | async-start | bytes 3276800 | tf_op jit(solution)/shard_map/reduce_scatter | solution.py:693
  174.4 278.1 %all-reduce.4.cloned.1.call-start = ((), (), s32[]{:S(2)}) async-start(), calls=%async_computation.15 | async-start | bytes 5120000 | tf_op jit(solution)/shard_map/psum | solution.py:694
  370.8 106.1 %reduce-scatter.19.cloned.1.call-start = ((), (), s32[]{:S(2)}) async-start(), calls=%async_computation.14 | async-start | bytes 614400
  372.6 129.0 %all-gather.6.cloned.1.call-start = ((), (), s32[]{:S(2)}) async-start(), calls=%async_computation.11 | async-start | bytes 1843200 | tf_op jit(solution)/shard_map/all_gather | solution.py:697
  452.5 40.4 %copy-start.5 = (bf16[1,240,384]{2,1,0:T(8,128)(2,1)S(1)}, bf16[1,240,384]{2,1,0:T(8,128)(2,1)}, u32[]{:S(2)}) copy-start(bf16[1,240,384]{2,1,0:T(8,128)(2,1)} %get-tuple-element.69) | copy-start | bytes 552964
  452.5 52.1 %all-gather.4.cloned.1.call-start = ((), (), s32[]{:S(2)}) async-start(), calls=%async_computation.9 | async-start | bytes 1843200 | tf_op jit(solution)/shard_map/all_gather | solution.py:697
  453.3 57.2 %all-gather.8.cloned.1.call-start = ((), (), s32[]{:S(2)}) async-start(), calls=%async_computation.13 | async-start | bytes 1966080 | tf_op jit(solution)/shard_map/all_gather | solution.py:697
  495.2 1.1 copy-start.4
  512.1 2.1 copy-start.3
  512.2 4.5 copy-start.1
  514.2 1.5 copy-start.2
Sparse Core Ops, SparseCore 0:
  147.5 22.2 reduce-scatter.10
  172.7 40.5 reduce-scatter.8
  216.1 48.8 reduce-scatter.14
  267.7 49.1 reduce-scatter.12
  319.0 51.6 reduce-scatter.16
  374.3 78.1 all-reduce.3
  455.4 21.4 reduce-scatter.18
  478.5 7.7 all-gather.5
  487.9 10.6 all-gather.3
  500.1 10.3 all-gather.7

commit v2 on v1

--- a/solution.py
+++ b/solution.py
@@ -1,5 +1,3 @@
-import functools
-
 import jax
 import jax.numpy as jnp
 from jax import lax
@@ -625,6 +623,529 @@
     )(ends, cosines, sines, seg_keys, seg_mine, gains, wq, wkv, wo, wg, wu, wd)
 
 
+def sums_kernel(
+    gain_sums, nf_h, in_h, gg_h, gu_h, br_h, la_h, ra_h, nr_h, kvg_h,
+    q_o, out_o, kv_o, gain_o, gate_o, up_o, down_o,
+    stage_a, stage_b, in_v, br_v, gg_v, gu_v, ra_v, kvg_v, nf_t, la_t, nr_t, in_t, gain_t,
+    d_out, d_in, d_keep, d1_out, d1_in, d2_out, d2_in,
+    f1_out, f1_in, f2_out, f2_in, f_keep, fz_in,
+    t1_out, t1_in, t2_out, t2_in, t_keep, tz_in,
+    d_all, f_all, t_all, gate_f, q_f, kv_f, gain_f, down_f,
+    load, dz_s, dz_r, d1_s, d1_r, d2_s, d2_r, f1_s, f1_r, f2_s, f2_r, fz_s, fz_r,
+    t1_s, t1_r, t2_s, t2_r, tz_s, tz_r, all_s, all_r, pair_r, write,
+):
+    section = lax.axis_index("section")
+    z = lax.axis_index("dp")
+    ctx = lax.axis_index("ctx")
+    x, y = ctx % 2, ctx // 2
+    x_next = (section, z, 2 * y + 1 - x)
+    y_next = (section, z, 2 * (1 - y) + x)
+    partner = (1 - section, z, ctx)
+    depth = nf_h.shape[0]
+    width = nf_h.shape[1]
+    per = width // RANKS
+    part = f_keep.shape[2]
+    shift = per - part
+    quarter = gg_v.shape[1] // 2
+    deep = in_h.shape[1] // RANKS
+    fine = deep // 2
+    last = RANKS - 1
+
+    def remote(src, dst, send, recv, device):
+        return pltpu.make_async_remote_copy(
+            src_ref=src, dst_ref=dst, send_sem=send, recv_sem=recv,
+            device_id=device, device_id_type=MESH,
+        )
+
+    def some(start, size, unit=16):
+        return pl.ds(pl.multiple_of(start, unit), size)
+
+    loads = [
+        pltpu.make_async_copy(h, v, load.at[i])
+        for i, (h, v) in enumerate(
+            [(in_h, in_v), (br_h, br_v), (nf_h, stage_a), (gg_h, gg_v), (gu_h, gu_v),
+             (la_h, stage_b), (ra_h, ra_v), (kvg_h, kvg_v), (nr_h, stage_a)]
+        )
+    ]
+    for copy in loads[:8]:
+        copy.start()
+    barrier = pltpu.get_barrier_semaphore()
+    for device in (x_next, y_next, partner):
+        pl.semaphore_signal(barrier, inc=1, device_id=device, device_id_type=MESH)
+    inner_left = (z > 0).astype(jnp.int32)
+    inner_right = (z < last).astype(jnp.int32)
+
+    @pl.when(z > 0)
+    def _():
+        pl.semaphore_signal(barrier, inc=1, device_id=(section, z - 1, ctx), device_id_type=MESH)
+
+    @pl.when(z < last)
+    def _():
+        pl.semaphore_signal(barrier, inc=1, device_id=(section, z + 1, ctx), device_id_type=MESH)
+
+    pl.semaphore_wait(barrier, 3 + inner_left + inner_right)
+
+    def turn(src, dst):
+        for at, size in tiles(src.shape[1], 128):
+            block = src[:, at : at + size]
+            if size < 128:
+                block = wide(block)
+            dst[at : at + size, :] = block.T[:size]
+
+    def z_way(t):
+        up = (z < t).astype(jnp.int32)
+        to = z + 2 * up - 1
+        arrives = up * inner_left + (1 - up) * inner_right
+        meets = (1 - up) * (t == z - 1).astype(jnp.int32)
+        return (section, to, ctx), arrives, t * (1 - meets) + RANKS * meets
+
+    def d_turn(k):
+        is_ = lambda v: (z == v).astype(jnp.int32)
+        order = ((3, 2, 1), (3, 0, 2), (0, 3, 1), (0, 1, 2))
+        return sum(is_(v) * order[v][k] for v in range(RANKS))
+
+    def d_block(t):
+        for b in range(deep // 128):
+            in_t[b * 128 : (b + 1) * 128, :] = in_v[:, some(t * deep + b * 128, 128, 128)].T
+
+    def d_send(k, t, sub):
+        device, _, slot = z_way(t)
+        rows = pl.ds(sub * fine, fine)
+        return remote(d_out.at[k, rows], d_in.at[slot, rows], dz_s.at[k, sub], dz_r.at[slot, sub], device)
+
+    def d_step(k):
+        t = d_turn(k)
+        _, arrives, _ = z_way(t)
+        d_block(t)
+        for sub in range(2):
+            rows = slice(sub * fine, (sub + 1) * fine)
+            mine = dot(in_t[rows, :], br_v[...])
+
+            @pl.when(arrives == 0)
+            def _():
+                d_out[k, rows, :] = mine.astype(BF16)
+
+            @pl.when(arrives == 1)
+            def _():
+                remote(d_out.at[k, rows], d_in.at[t, rows], dz_s.at[k, sub], dz_r.at[t, sub], partner).wait_recv()
+                d_out[k, rows, :] = (mine + d_in[t, rows, :].astype(F32)).astype(BF16)
+
+            d_send(k, t, sub).start()
+
+    def f_links(k):
+        return (x_next, y_next, x, y) if k == 0 else (y_next, x_next, y, x)
+
+    def f_right(k, column_half):
+        src = gg_v if k == 0 else gu_v
+        return src[:, some(column_half * quarter, quarter, 128)]
+
+    def f1_copy(k, d):
+        return remote(f1_out.at[k, d], f1_in.at[k, d], f1_s.at[k, d], f1_r.at[k, d], f_links(k)[0])
+
+    def f2_copy(k, d):
+        return remote(f2_out.at[k, d], f2_in.at[k, d], f2_s.at[k, d], f2_r.at[k, d], f_links(k)[1])
+
+    def f1_step(d):
+        for k in range(2):
+            first = f_links(k)[2]
+            left = nf_t[some(d * per, per), :]
+            f1_out[k, d] = dot(left, f_right(k, 1 - first)).astype(BF16)
+            f1_copy(k, d).start()
+
+    def f2_step(d):
+        for k in range(2):
+            first, second = f_links(k)[2:]
+            f1_copy(k, d).wait_recv()
+            for mine in (False, True):
+                at = (second if mine else 1 - second) * shift
+                total = dot(nf_t[some(d * per + at, part), :], f_right(k, first)) + f1_in[
+                    k, d, some(at, part), :
+                ].astype(F32)
+                if mine:
+                    f_keep[k, d] = total.astype(BF16)
+                else:
+                    f2_out[k, d] = total.astype(BF16)
+                    f2_copy(k, d).start()
+
+    def t_links(d):
+        x_first = (d < RANKS // 2).astype(jnp.int32)
+        first, second = x_first * x + (1 - x_first) * y, x_first * y + (1 - x_first) * x
+        to_x = (section, z, 2 * y + 1 - x)
+        to_y = (section, z, 2 * (1 - y) + x)
+        pick = lambda a, b: tuple(x_first * i + (1 - x_first) * j for i, j in zip(a, b))
+        return pick(to_x, to_y), pick(to_y, to_x), first, second
+
+    def t_product(row, count, add):
+        mine = dot(la_t[some(row, count), :], ra_v[...])
+        pairs = dot(nr_t[some(row, count), :], kvg_v[...])
+        gains = gain_t[some(row, count), :]
+        full = width // 128 * 128
+        tail = jnp.concatenate([mine[:, full:], gains[:, width - full :]], axis=1)
+        return [(0, add(mine[:, :full], 0)), (full, add(tail, full)), (full + 128, add(pairs, full + 128))]
+
+    def t1_copy(d):
+        return remote(t1_out.at[d], t1_in.at[d], t1_s.at[d], t1_r.at[d], t_links(d)[0])
+
+    def t2_copy(d):
+        return remote(t2_out.at[d], t2_in.at[d], t2_s.at[d], t2_r.at[d], t_links(d)[1])
+
+    def t1_step(d):
+        first = t_links(d)[2]
+        for at, value in t_product(d * per + (1 - first) * shift, part, lambda v, at: v):
+            t1_out[d, :, at : at + value.shape[1]] = value.astype(BF16)
+        t1_copy(d).start()
+
+    def t2_step(d):
+        _, _, first, second = t_links(d)
+        t1_copy(d).wait_recv()
+        for mine in (False, True):
+            row = (second if mine else 1 - second) * (part // 2)
+            add = lambda v, at: v + t1_in[d, some(row, part // 2), at : at + v.shape[1]].astype(F32)
+            dst = t_keep if mine else t2_out
+            for at, value in t_product(d * per + first * shift + row, part // 2, add):
+                dst[d, :, at : at + value.shape[1]] = value.astype(BF16)
+            if not mine:
+                t2_copy(d).start()
+
+    def z_step(keep, second_in, z_in, send, recv, copy, d):
+        copy.wait_recv()
+        keep[d] = (keep[d].astype(F32) + second_in[d].astype(F32)).astype(BF16)
+
+        @pl.when(z != d)
+        def _():
+            device, arrives, slot = z_way(d)
+
+            @pl.when(arrives == 1)
+            def _():
+                remote(keep.at[d], z_in.at[d], send.at[d], recv.at[d], partner).wait_recv()
+                keep[d] = (keep[d].astype(F32) + z_in[d].astype(F32)).astype(BF16)
+
+            remote(keep.at[d], z_in.at[slot], send.at[d], recv.at[slot], device).start()
+
+    def z_arrived(z_in, recv, src):
+        @pl.when(z > 0)
+        def _():
+            remote(src, z_in.at[z], recv.at[z], recv.at[z], partner).wait_recv()
+
+        @pl.when(z < last)
+        def _():
+            remote(src, z_in.at[RANKS], recv.at[RANKS], recv.at[RANKS], partner).wait_recv()
+
+    def z_total(value, up, down):
+        value = value + jnp.where(z > 0, up.astype(F32), 0.0)
+        return value + jnp.where(z < last, down.astype(F32), 0.0)
+
+    def places(x_first):
+        a, b = (1, 0) if x_first is True else (0, 1) if x_first is False else (x_first, 1 - x_first)
+        spot = lambda i, j: a * (2 * i + j) + b * (2 * j + i)
+        return spot(x, y), spot(1 - x, y), spot(x, 1 - y), spot(1 - x, 1 - y)
+
+    class Gather:
+        def __init__(self, number, buffer, x_first):
+            self.n, self.buffer = number, buffer
+            self.own, self.over_x, self.over_y, self.across = places(x_first)
+            rows = buffer.shape[2]
+            cut = (rows // 2 + 15) // 16 * 16
+            self.halves = (pl.ds(0, cut), pl.ds(cut, rows - cut))
+
+        def whole(self, spot, slot, device):
+            ref = self.buffer.at[section, spot]
+            return remote(ref, ref, all_s.at[self.n, slot], all_r.at[self.n, slot], device)
+
+        def relay(self, spot, half, device):
+            ref = self.buffer.at[section, spot, self.halves[half]]
+            return remote(ref, ref, all_s.at[self.n, 2 + half], all_r.at[self.n, 2 + half], device)
+
+        def pair(self, core, spot, slot):
+            ref = self.buffer.at[core, spot]
+            return remote(ref, ref, all_s.at[self.n, 4 + slot], pair_r.at[self.n, spot], partner)
+
+        def start(self):
+            self.whole(self.own, 0, x_next).start()
+            self.whole(self.own, 1, y_next).start()
+            self.pair(section, self.own, 0).start()
+
+        def middle(self):
+            self.whole(self.over_x, 0, x_next).wait_recv()
+            self.relay(self.over_x, 0, y_next).start()
+            self.pair(section, self.over_x, 1).start()
+            self.whole(self.over_y, 1, y_next).wait_recv()
+            self.relay(self.over_y, 1, x_next).start()
+            self.pair(section, self.over_y, 2).start()
+
+        def finish(self):
+            self.relay(self.across, 0, y_next).wait_recv()
+            self.relay(self.across, 1, x_next).wait_recv()
+            self.pair(section, self.across, 3).start()
+            for spot in (self.own, self.over_x, self.over_y, self.across):
+                self.pair(1 - section, spot, 0).wait_recv()
+
+        def sent(self):
+            self.whole(self.own, 0, x_next).wait_send()
+            self.whole(self.own, 1, y_next).wait_send()
+            self.relay(self.over_x, 0, y_next).wait_send()
+            self.relay(self.over_y, 1, x_next).wait_send()
+            for slot, spot in enumerate((self.own, self.over_x, self.over_y, self.across)):
+                self.pair(section, spot, slot).wait_send()
+
+    below = (z < RANKS // 2).astype(jnp.int32)
+    gathers = [
+        Gather(0, d_all.at[0], True),
+        Gather(1, d_all.at[1], False),
+        Gather(2, f_all.at[0], True),
+        Gather(3, f_all.at[1], False),
+        Gather(4, t_all, below),
+    ]
+
+    def in_order(i):
+        odd = i % 2
+        return (1 - odd) * (last - i // 2) + odd * (i // 2)
+
+    def each(step):
+        def body(i, carry):
+            step(in_order(i))
+            return carry
+
+        lax.fori_loop(0, RANKS, body, 0)
+
+    loads[0].wait()
+    loads[1].wait()
+    d_step(0)
+    loads[2].wait()
+    turn(stage_a, nf_t)
+    loads[8].start()
+    loads[3].wait()
+    loads[4].wait()
+    each(f1_step)
+    d_step(1)
+    loads[5].wait()
+    turn(stage_b, la_t)
+    loads[8].wait()
+    turn(stage_a, nr_t)
+    loads[6].wait()
+    loads[7].wait()
+    gain_rows = jnp.concatenate(
+        [gain_sums[...], jnp.zeros((128 - gain_sums.shape[0], width), F32)], axis=0
+    )
+    for at, size in tiles(width, 128):
+        block = wide(gain_rows[:, at : at + size]).T
+        gain_t[at : at + size, :] = pltpu.roll(block, 64, 1)[:size]
+    each(t1_step)
+    d_step(2)
+    each(f2_step)
+
+    d_block(z)
+
+    def d1_copy(h):
+        return remote(d1_out.at[h], d1_in.at[h], d1_s.at[h], d1_r.at[h], f_links(h)[0])
+
+    def d2_copy(h):
+        return remote(d2_out.at[h], d2_in.at[h], d2_s.at[h], d2_r.at[h], f_links(h)[1])
+
+    for h in range(2):
+        rows = slice(h * fine, (h + 1) * fine)
+
+        @pl.when(z > 0)
+        def _():
+            remote(d_out.at[0, rows], d_in.at[z, rows], dz_r.at[z, h], dz_r.at[z, h], partner).wait_recv()
+
+        @pl.when(z < last)
+        def _():
+            remote(d_out.at[0, rows], d_in.at[RANKS, rows], dz_r.at[RANKS, h], dz_r.at[RANKS, h], partner).wait_recv()
+
+        first = f_links(h)[2]
+        for mine in (False, True):
+            at = h * fine + (first if mine else 1 - first) * (fine // 2)
+            span = some(at, fine // 2)
+            total = z_total(dot(in_t[span, :], br_v[...]), d_in[z, span, :], d_in[RANKS, span, :])
+            if mine:
+                d_keep[h] = total
+            else:
+                d1_out[h] = total.astype(BF16)
+                d1_copy(h).start()
+
+    each(t2_step)
+    each(lambda d: [
+        z_step(f_keep.at[k], f2_in.at[k], fz_in.at[k], fz_s.at[k], fz_r.at[k], f2_copy(k, d), d)
+        for k in range(2)
+    ])
+    for h in range(2):
+        second = f_links(h)[3]
+        d1_copy(h).wait_recv()
+        for mine in (False, True):
+            span = some((second if mine else 1 - second) * (fine // 4), fine // 4)
+            total = d_keep[h, span, :] + d1_in[h, span, :].astype(F32)
+            if mine:
+                d_keep[h, : fine // 4, :] = total
+            else:
+                d2_out[h] = total.astype(BF16)
+                d2_copy(h).start()
+    each(lambda d: z_step(t_keep, t2_in, tz_in, tz_s, tz_r, t2_copy(d), d))
+    for h in range(2):
+        d2_copy(h).wait_recv()
+        gathers[h].buffer[section, gathers[h].own] = (
+            d_keep[h, : fine // 4, :] + d2_in[h].astype(F32)
+        ).astype(BF16)
+        gathers[h].start()
+    for k in range(2):
+        z_arrived(fz_in.at[k], fz_r.at[k], f_keep.at[k, 0])
+        f_all[k, section, gathers[2 + k].own] = z_total(
+            f_keep[k, z].astype(F32), fz_in[k, z], fz_in[k, RANKS]
+        ).astype(BF16)
+        gathers[2 + k].start()
+    gathers[0].middle()
+    gathers[1].middle()
+    z_arrived(tz_in, tz_r, t_keep.at[0])
+    t_all[section, gathers[4].own] = z_total(
+        t_keep[z].astype(F32), tz_in[z], tz_in[RANKS]
+    ).astype(BF16)
+    gathers[4].start()
+    gathers[2].middle()
+    gathers[3].middle()
+
+    half_columns = 2 * quarter
+    gathers[0].finish()
+    gathers[1].finish()
+    for core in range(2):
+        columns = slice(512 * core, min(512 * core + 512, width))
+        for h in range(2):
+            for spot in range(4):
+                row = h * fine + spot * (fine // 4)
+                down_f[row : row + fine // 4, columns] = d_all[h, core, spot][
+                    :, : columns.stop - columns.start
+                ].astype(F32)
+    writes = [pltpu.make_async_copy(down_f, down_o, write.at[0])]
+    writes[0].start()
+    gathers[4].middle()
+    for k in range(2):
+        gathers[2 + k].finish()
+        for core in range(2):
+            for f in range(2):
+                at = core * half_columns + f * quarter
+                columns = slice(at, at + quarter)
+                gate_f[k, :part, columns] = f_all[k, core, 2 * f].astype(F32)
+                gate_f[k, part:, columns] = f_all[k, core, 2 * f + 1, part - shift :, :].astype(F32)
+        writes.append(pltpu.make_async_copy(gate_f.at[k], (gate_o, up_o)[k], write.at[1 + k]))
+        writes[-1].start()
+    gathers[4].finish()
+    t_rows = part // 2
+    pairs_at = width // 128 * 128 + 128
+    for core in range(2):
+        for spot in range(4):
+            row = spot % 2 * t_rows + spot // 2 * shift
+            skip = part - shift if spot == 2 else 0
+            span = slice(row + skip, row + t_rows)
+            q_f[core, span, :] = t_all[core, spot, skip:, :width].astype(F32)
+            kv_f[core, span, :] = t_all[core, spot, skip:, pairs_at:].astype(F32)
+            gain = t_all[core, spot, skip:, pairs_at - 128 : pairs_at].astype(F32)
+            gain_f[span, :] = gain if core == 0 else gain_f[span, :] + gain
+    for i, (src, dst) in enumerate(
+        [(q_f.at[0], q_o), (q_f.at[1], out_o), (kv_f, kv_o), (gain_f, gain_o)]
+    ):
+        writes.append(pltpu.make_async_copy(src, dst, write.at[3 + i]))
+        writes[-1].start()
+
+    for k in range(3):
+        for sub in range(2):
+            d_send(k, d_turn(k), sub).wait_send()
+    for h in range(2):
+        d1_copy(h).wait_send()
+        d2_copy(h).wait_send()
+
+    def sent(d):
+        t1_copy(d).wait_send()
+        t2_copy(d).wait_send()
+        for k in range(2):
+            f1_copy(k, d).wait_send()
+            f2_copy(k, d).wait_send()
+
+        @pl.when(z != d)
+        def _():
+            for keep, z_in, send in (
+                (f_keep.at[0], fz_in.at[0], fz_s.at[0]),
+                (f_keep.at[1], fz_in.at[1], fz_s.at[1]),
+                (t_keep, tz_in, tz_s),
+            ):
+                remote(keep.at[d], z_in.at[d], send.at[d], send.at[d], partner).wait_send()
+
+    each(sent)
+    for gather in gathers:
+        gather.sent()
+    for copy in writes:
+        copy.wait()
+
+
+def run_sums(gain_sums, operands):
+    nf, inner, gg, gu, br, la, ra, nr, kvg = operands
+    depth, width = nf.shape
+    ff, half = inner.shape[1], gg.shape[1]
+    per, deep = width // RANKS, ff // RANKS
+    part = (per // 2 + 15) // 16 * 16
+    quarter, fine = half // 2, deep // 2
+    columns = br.shape[1]
+    wide_t = width // 128 * 128 + 128 + kvg.shape[1]
+    vmem, hbm = pl.BlockSpec(memory_space=pltpu.VMEM), pl.BlockSpec(memory_space=pl.ANY)
+    out = lambda *shape: jax.ShapeDtypeStruct(shape, F32)
+    b = lambda *shape: pltpu.VMEM(shape, BF16)
+    f = lambda *shape: pltpu.VMEM(shape, F32)
+    sem = lambda *shape: pltpu.SemaphoreType.DMA(shape)
+    return pl.pallas_call(
+        sums_kernel,
+        out_shape=[
+            out(per, width), out(per, width), out(2, per, kvg.shape[1]), out(per, 128),
+            out(per, ff), out(per, ff), out(deep, width),
+        ],
+        in_specs=[vmem] + [hbm] * 9,
+        out_specs=[hbm] * 7,
+        scratch_shapes=[
+            b(depth, width), b(depth, width), b(depth, ff), b(depth, columns), b(depth, half), b(depth, half),
+            b(depth, width), b(depth, kvg.shape[1]),
+            b(width, depth), b(width, depth), b(width, depth), b(deep, depth), f(width, 128),
+            b(3, deep, columns), b(5, deep, columns), f(2, fine // 2, columns),
+            b(2, fine // 2, columns), b(2, fine // 2, columns), b(2, fine // 4, columns), b(2, fine // 4, columns),
+            b(2, RANKS, per, quarter), b(2, RANKS, per, quarter),
+            b(2, RANKS, part, quarter), b(2, RANKS, part, quarter), b(2, RANKS, part, quarter), b(2, 5, part, quarter),
+            b(RANKS, part, wide_t), b(RANKS, part, wide_t),
+            b(RANKS, part // 2, wide_t), b(RANKS, part // 2, wide_t), b(RANKS, part // 2, wide_t), b(5, part // 2, wide_t),
+            b(2, 2, 4, fine // 4, columns), b(2, 2, 4, part, quarter), b(2, 4, part // 2, wide_t),
+            f(2, per, ff), f(2, per, width), f(2, per, kvg.shape[1]), f(per, 128), f(deep, width),
+            sem(9), sem(3, 2), sem(5, 2), sem(2), sem(2), sem(2), sem(2),
+            sem(2, 4), sem(2, 4), sem(2, 4), sem(2, 4), sem(2, 4), sem(2, 5),
+            sem(4), sem(4), sem(4), sem(4), sem(4), sem(5),
+            sem(5, 8), sem(5, 4), sem(5, 4), sem(7),
+        ],
+        compiler_params=pltpu.CompilerParams(
+            collective_id=2, has_side_effects=True, vmem_limit_bytes=61 * 2**20
+        ),
+        name="sums",
+    )(gain_sums, *operands)
+
+
+def sums_by_xla(gain_sums, operands):
+    nf, inner, gg, gu, br, la, ra, nr, kvg = operands
+    width = nf.shape[1]
+
+    def reduced(left, right):
+        total = dot_lt(left, right).astype(BF16)
+        piece = lax.psum_scatter(total, "dp", scatter_dimension=0, tiled=True)
+        return lax.psum(piece, "ctx")
+
+    def both(piece, axis):
+        return lax.all_gather(piece, "section", axis=axis, tiled=axis > 0).astype(F32)
+
+    attn = both(reduced(la, ra), 0)
+    gain_sum = lax.psum(gain_sums[:2], ("section", "ctx"))
+    return (
+        attn[0],
+        attn[1],
+        both(reduced(nr, kvg), 0),
+        lax.psum_scatter(gain_sum, "dp", scatter_dimension=1, tiled=True),
+        both(reduced(nf, gg), 1),
+        both(reduced(nf, gu), 1),
+        both(reduced(inner, br), 1)[:, :width],
+    )
+
+
 def shards(
     ends,
     doc_lengths,
@@ -686,35 +1207,30 @@
         (w_query, w_kv, w_out, w_gate, w_up, w_down),
     )
 
-    def reduced(left, right):
-        total = lax.dot_general(
-            left, right, (((0,), (0,)), ((), ())), preferred_element_type=F32
-        ).astype(BF16)
-        piece = lax.psum_scatter(total, "dp", scatter_dimension=0, tiled=True)
-        return lax.psum(piece, "ctx")
-
-    def both(piece, axis):
-        return lax.all_gather(piece, "section", axis=axis, tiled=axis > 0).astype(F32)
-
-    grad_gate = both(reduced(nf, gg), 1)
-    grad_up = both(reduced(nf, gu), 1)
-    grad_down = both(reduced(inner, br), 1)[:, :width]
-    attn = both(reduced(la, ra), 0)
-    kv_parts = both(reduced(nr, kvg), 0)
+    operands = (nf, inner, gg, gu, br, la, ra, nr, kvg)
+    fits = lax.axis_size("dp") == RANKS and width % 64 == 0 and inner.shape[1] % 1280 == 0
+    if fits:
+        grad_query, grad_out, kv_parts, gain_pieces, grad_gate, grad_up, grad_down = run_sums(
+            gain_sums, operands
+        )
+        gain_at = width % 128
+        gain_piece = gain_pieces[:, gain_at : gain_at + 2].T
+    else:
+        grad_query, grad_out, kv_parts, gain_piece, grad_gate, grad_up, grad_down = sums_by_xla(
+            gain_sums, operands
+        )
     kv_grad = jnp.concatenate([kv_parts[0], kv_parts[1][:, 128:]], axis=1).reshape(
         -1, KEY_VALUE_HEADS, 2, HEAD_SIZE
     )
     grad_key = kv_grad[:, :, 0].reshape(kv_grad.shape[0], -1)
     grad_value = kv_grad[:, :, 1].reshape(kv_grad.shape[0], -1)
-    gain_sum = lax.psum(gain_sums[:2], ("section", "ctx"))
-    gain_piece = lax.psum_scatter(gain_sum, "dp", scatter_dimension=1, tiled=True)
     return (
         acts,
         grads_in,
-        attn[0],
+        grad_query,
         grad_key,
         grad_value,
-        attn[1],
+        grad_out,
         grad_gate,
         grad_up,
         grad_down,

time: 525 us -> 276 us (0.53)
  waiting for transfers between devices: 303 us -> 0 us
  Pallas kernels: 117 us -> 237 us
  matrix products: 27.5 us -> 0 us
  blocking collectives: 19.5 us -> 0 us
  between operations: 15.7 us -> 2.08 us
  other arithmetic: 13.1 us -> 6.03 us
    reduce_scatter x5 -> x0, waiting for transfers between devices: 196 us -> none  [reduced(): piece = lax.psum_scatter(total, 'dp', scatter_dimension=0, tiled=True)]
    pallas_call x0 -> x1, Pallas kernels: none -> 120 us  [run_sums(): pl.pallas_call(sums_kernel, out_shape=[out(per, width), out(per, width),...]
    psum x1 -> x0, waiting for transfers between devices: 79.9 us -> none  [reduced(): return lax.psum(piece, 'ctx')]
    dot_general x5 -> x0, matrix products: 27.5 us -> none  [reduced(): lax.dot_general(left, right, (((0,), (0,)), ((), ())), preferred_element_...]
    unnamed x11 -> x0, waiting for transfers between devices: 24.4 us -> none
    psum x1 -> x0, blocking collectives: 14.4 us -> none  [shards(): gain_sum = lax.psum(gain_sums[:2], ('section', 'ctx'))]
    convert_element_type x4 -> x0, other arithmetic: 6.3 us -> none  [both(): lax.all_gather(piece, 'section', axis=axis, tiled=axis > 0).astype(F32)]
  transfers between devices with their start and end apart: 10 -> 0, of which waited for: 7 -> 0; matrix products, arithmetic and copies ran while one was open for 7% -> 0% of each run, Pallas kernels for 0% -> 0%
where the time goes in v2:
time: 276 us; the launch traced here: 275 us
  Pallas kernels  237 us (86%)
  local copies, waits for them, and re-layouts  30.2 us (11%)
  other arithmetic  6.03 us (2%)
    pallas_call x1, Pallas kernels, run_sums(): pl.pallas_call(sums_kernel, out_shape=[out(per, width), out(per, width),...  120 us
    pallas_call x1, Pallas kernels, run_layers(): pl.pallas_call(layers_kernel, out_shape=[out(*ends.shape), out(*ends.shap...  117 us
    unnamed x24, local copies, waits for them, and re-layouts  20.2 us

profile of v2, /device:TPU:0, one launch (start us, length us, event | category | flops | bytes accessed | tf_op | source)
XLA Modules:
  0.0 275.2 jit_solution(1220418439698947322)
XLA Ops:
  0.6 0.0 copy-start
  0.7 0.6 copy-done
  1.3 0.6 fusion.8
  3.2 1.3 convert_add_fusion.1
  4.6 0.7 convert_add_fusion
  5.2 0.7 stack.12
  5.9 0.7 stack.13
  6.6 0.6 fusion.4.gains
  7.2 0.6 iota.46.seg_keys
  7.8 0.7 iota.47.seg_mine
  8.6 1.2 sine_multiply_fusion
  9.7 1.4 pad_maximum_fusion
  11.1 1.4 copy.30.wkv_h
  12.6 7.9 %copy.31.wd_h = bf16[2560,960]{1,0:T(8,128)(2,1)} copy(bf16[2560,960]{0,1:T(8,128)(2,1)} %param.19) | data formatting | bytes 9830400 | tf_op args[8]
  20.5 117.2 %layers.1 = (bf16[1,2,224,960]{3,2,1,0:T(8,128)(2,1)}, bf16[1,2,224,960]{3,2,1,0:T(8,128)(2,1)}, f32[8,960]{1,0:T(8,128)}, bf16[896,960]{1,0:T(8,128)(2,1)}, bf1...) custom-call(bf16[1,2,224,960]{3,2,1,0:T(8,128)(2,1)} %ends.1, ...), custom_call_target="tpu_custom_call" | custom-call | tf_op jit(solution)/shard_map/layers/pallas_call | solution.py:559
  137.7 119.7 %sums.1 = (f32[240,960]{1,0:T(8,128)}, f32[240,960]{1,0:T(8,128)}, f32[2,240,384]{2,1,0:T(8,128)}, f32[240,128]{1,0:T(8,128)}, f32[240,2560]{1,0:T(8,128)}, /*index=5*/f32[240,2560]{1,0:T(8,128)}, f32[640,960]{1,0:T(8,128)}) custom-call(f32[8,960]{1,0:T(8,128)} %get-tuple-element.32.gain_sums, bf16[896,960]{1,0:T(8,128)(2,1)} %get-tuple-element.33.nf_h, ...), custom_call_target="tpu_custom_call" | custom-call | tf_op jit(solution)/shard_map/sums/pallas_call | solution.py:1092
  257.4 1.0 slice_bitcast_fusion.2
  258.4 0.8 slice_reduce_fusion
  259.2 1.1 slice_bitcast_fusion.1
  260.4 0.9 pad_maximum_fusion.1
  261.3 1.4 copy.32
  262.7 0.9 fusion.7
  263.6 2.0 copy.33
  265.6 2.2 copy.40
  267.9 0.9 copy.41
  268.8 0.9 copy.42
  269.7 0.0 copy-done.5
  269.7 0.9 copy.43
  270.7 0.5 copy-done.4
  271.2 1.4 copy.44
  272.7 1.1 copy-done.3
  273.8 1.4 copy.45
  (16 shorter events, 0.1 us)
Async XLA Ops:
  0.6 0.7 copy-start
  260.4 3.2 %copy-start.2 = (f32[640,960]{1,0:T(8,128)S(1)}, f32[640,960]{1,0:T(8,128)}, u32[]{:S(2)}) copy-start(f32[640,960]{1,0:T(8,128)} %get-tuple-element.68) | copy-start | bytes 7372804
  263.6 4.3 %copy-start.7 = (bf16[1,2,224,960]{3,2,1,0:T(8,128)(2,1)S(1)}, bf16[1,2,224,960]{3,2,1,0:T(8,128)(2,1)}, u32[]{:S(2)}) copy-start(bf16[1,2,224,960]{3,2,1,0:T(8,128)(2,1)} %get-tuple-element.101) | copy-start | bytes 2580484
  265.6 3.2 %copy-start.6 = (f32[240,960]{1,0:T(8,128)S(1)}, f32[240,960]{1,0:T(8,128)}, u32[]{:S(2)}) copy-start(f32[240,960]{1,0:T(8,128)} %get-tuple-element.102) | copy-start | bytes 2764804
  267.9 1.9 copy-start.5
  268.8 2.4 copy-start.4
  271.2 2.6 copy-start.3
  271.2 4.0 %copy-start.1 = (s32[2,1,2]{2,1,0:T(1,128)S(1)}, s32[2,1,2]{2,1,0:T(1,128)}, u32[]{:S(2)}) copy-start(s32[2,1,2]{2,1,0:T(1,128)} %param.12) | copy-start | bytes 52

commit v3 on v2

--- a/solution.py
+++ b/solution.py
@@ -1,5 +1,6 @@
 import jax
 import jax.numpy as jnp
+import numpy as np
 from jax import lax
 from jax.experimental import pallas as pl
 from jax.experimental.pallas import tpu as pltpu
@@ -54,12 +55,12 @@
 
 
 def layers_kernel(
-    ends, cosines, sines, seg_keys, seg_mine, gains, wq_h, wkv_h, wo_h, wg_h, wu_h, wd_h,
+    lengths, ends, frequency, gain_a, gain_f, wq_h, wk_h, wv_h, wo_h, wg_h, wu_h, wd_h,
     acts_o, grads_o, gain_o, nf_o, in_o, gg_o, gu_o, br_o, la_o, ra_o, nr_o, kvg_o,
     wq, wkv, wo, wg, wu, wd,
     act, go, middle, norm_ffn, fact_a, fact_b, inner, lm, qd, kv, o_raw,
-    sum_acc, gm, gg, gu, br, ra, dq_raw, pds, dkv, dkv_in, gkv,
-    w_sem, in_send, in_recv, kv_send, kv_recv, dk_send, dk_recv, out_send, out_recv,
+    sum_acc, gm, gg, gu, br, ra, dq_raw, pds, dkv, dkv_in, gkv, cos_sin, allowed_add,
+    w_sem, kv_sem, in_send, in_recv, kv_send, kv_recv, dk_send, dk_recv, out_send, out_recv,
     op_own, op_send, op_recv,
 ):
     section = lax.axis_index("section")
@@ -79,10 +80,19 @@
 
     loads = [
         pltpu.make_async_copy(h, v, w_sem.at[i])
-        for i, (h, v) in enumerate(
-            [(wkv_h, wkv), (wq_h, wq), (wo_h, wo), (wg_h, wg), (wu_h, wu), (wd_h, wd)]
+        for i, (h, v) in enumerate([(wq_h, wq), (wo_h, wo), (wg_h, wg), (wu_h, wu), (wd_h, wd)])
+    ]
+    kv_loads = [
+        pltpu.make_async_copy(
+            h.at[pl.ds(g * HEAD_SIZE, HEAD_SIZE)],
+            wkv.at[pl.ds((2 * g + i) * HEAD_SIZE, HEAD_SIZE)],
+            kv_sem.at[i, g],
         )
+        for g in range(KEY_VALUE_HEADS)
+        for i, h in enumerate((wk_h, wv_h))
     ]
+    for load in kv_loads + loads:
+        load.start()
     kv[...] = jnp.zeros_like(kv)
     barrier = pltpu.get_barrier_semaphore()
     for step in range(1, 8):
@@ -110,34 +120,46 @@
     def in_mine(block):
         return (section == ctx // 2) & (ctx // 2 == block)
 
-    for block in range(2):
-        for into_x in (True, False):
-            here = section == (0 if into_x else 1)
-            local, remote = in_copy(block, into_x)
+    def in_start(into_x):
+        here = section == (0 if into_x else 1)
+        for block in range(2):
 
             @pl.when(here & in_mine(block))
-            def _(local=local):
-                local.start()
+            def _(block=block):
+                in_copy(block, into_x)[0].start()
 
             @pl.when(here & jnp.logical_not(in_mine(block)))
-            def _(remote=remote):
-                remote.start()
-
-    for load in loads:
-        load.start()
+            def _(block=block):
+                in_copy(block, into_x)[1].start()
+
+    in_start(True)
 
     lane = lanes(rows)
     low = lane < HEAD_SIZE
-    cos_q = cosines[...]
-    sin_q = sines[...]
-    gain_attn = gains[0:1, :]
-    gain_ffn = gains[1:2, :]
-
-    def mask():
-        query_index = rank * rows + lax.broadcasted_iota(jnp.int32, (rows, RANKS * rows), 0)
-        key_index = lax.broadcasted_iota(jnp.int32, (rows, RANKS * rows), 1)
-        ok = (seg_mine[:, 0:1] == seg_keys[0:1, :]) & (query_index >= key_index)
-        return jnp.where(ok, 0.0, masked_fill)
+    gain_attn = gain_a[...].astype(F32)
+    gain_ffn = gain_f[...].astype(F32)
+
+    def place(token_index):
+        segment = jnp.zeros_like(token_index)
+        start = jnp.zeros_like(token_index)
+        finish = jnp.int32(0)
+        for slot in range(lengths.shape[2]):
+            length = lengths[micro, 0, slot]
+            finish = finish + length
+            passed = (token_index >= finish).astype(jnp.int32)
+            segment = segment + passed
+            start = start + passed * length
+        return segment, token_index - start
+
+    seg_mine, position = place(rank * rows + lax.broadcasted_iota(jnp.int32, (rows, 128), 0))
+    angles = position.astype(F32) * frequency[...]
+    cos_sin[0] = jnp.cos(angles)
+    cos_sin[1] = jnp.where(lane % HEAD_SIZE < HEAD_SIZE // 2, -1.0, 1.0) * jnp.sin(angles)
+    key_index = lax.broadcasted_iota(jnp.int32, (1, RANKS * rows), 1)
+    query_index = rank * rows + lax.broadcasted_iota(jnp.int32, (rows, 1), 0)
+    allowed_add[...] = jnp.where(
+        (seg_mine[:, 0:1] == place(key_index)[0]) & (query_index >= key_index), 0.0, masked_fill
+    )
 
     def kv_rows(l, r):
         return kv.at[l, pl.ds(pl.multiple_of(r * rows, 16), rows)]
@@ -251,40 +273,27 @@
             op_copy(kind, l, True).wait()
             op_copy(kind, l, False).wait_send()
 
-    @pl.when(section == 0)
-    def _():
-        for block in range(2):
-
-            @pl.when(jnp.logical_not(in_mine(block)))
-            def _(block=block):
-                in_copy(block, True)[1].wait_send()
-
-    @pl.when(section == 1)
-    def _():
-        for block in range(2):
-
-            @pl.when(jnp.logical_not(in_mine(block)))
-            def _(block=block):
-                in_copy(block, False)[1].wait_send()
-
     in_copy(0, True)[1].wait_recv()
-    loads[0].wait()
+    for load in kv_loads:
+        load.wait()
 
     def forward(l, carry):
         hidden = act[l].astype(F32)
+        cos_q, sin_q = cos_sin[0], cos_sin[1]
         lm[l, 0] = (hidden * inverse_rms(hidden) * gain_attn).astype(BF16)
         cos_kv = jnp.where(low, cos_q, 1.0)
         sin_kv = jnp.where(low, sin_q, 0.0)
         mine = pl.ds(pl.multiple_of(rank * rows, 16), rows)
         for g in range(KEY_VALUE_HEADS):
-            block = dot(lm[l, 0], wkv[:, 128 * g : 128 * g + 128])
+            block = dot_rt(lm[l, 0], wkv[128 * g : 128 * g + 128, :])
             turned = block * cos_kv + half_turn(block) * sin_kv
             kv[l, mine, 128 * g : 128 * g + 128] = turned.astype(BF16)
         kv_start(l)
 
         @pl.when(l == 0)
         def _():
-            loads[1].wait()
+            loads[0].wait()
+            in_start(False)
 
         for at, size in tiles(width, 256):
             product = dot(lm[l, 0], wq[:, at : at + size])
@@ -301,7 +310,8 @@
                         low, pltpu.roll(turned, 64, 1), 0.0
                     ).astype(BF16)
         kv_finish(l)
-        allowed = mask()
+        allowed = allowed_add[...]
+        cos_q, sin_q = cos_sin[0], cos_sin[1]
 
         def heads(g, carry):
             kv_g = kv[l, :, pl.ds(pl.multiple_of(g * 128, 128), 128)]
@@ -324,7 +334,7 @@
 
         @pl.when(l == 0)
         def _():
-            loads[2].wait()
+            loads[1].wait()
 
         for at, size in tiles(width, 256):
             middle[l, :, at : at + size] = act[l, :, at : at + size].astype(F32) + dot(
@@ -335,8 +345,8 @@
 
         @pl.when(l == 0)
         def _():
+            loads[2].wait()
             loads[3].wait()
-            loads[4].wait()
 
         def gates(j, carry):
             part = pl.ds(pl.multiple_of(j * 256, 256), 256)
@@ -353,11 +363,11 @@
 
         @pl.when(l == 0)
         def _():
-            loads[5].wait()
+            loads[4].wait()
 
         for at, size in tiles(width, 256):
             act[l + 1, :, at : at + size] = (
-                middle[l, :, at : at + size] + dot(inner[l], wd[:, at : at + size])
+                middle[l, :, at : at + size] + dot_rt(inner[l], wd[at : at + size, :])
             ).astype(BF16)
         out_start(act.at[l + 1], acts_o, l, 0)
         op_start((0, 1, 7), l)
@@ -393,7 +403,7 @@
 
         def gates(j, carry):
             part = pl.ds(pl.multiple_of(j * 256, 256), 256)
-            grad_inner = dot_rt(go[l + 1], wd[part, :])
+            grad_inner = dot(go[l + 1], wd[:, part])
             gg[:, part] = (grad_inner * fact_a[l, :, part].astype(F32)).astype(BF16)
             gu[:, part] = (grad_inner * fact_b[l, :, part].astype(F32)).astype(BF16)
             return carry
@@ -429,7 +439,8 @@
                     qd[l, head // SHARE, pl.ds((SHARE + head % SHARE) * rows, rows), :] = (
                         jnp.where(low, 0.0, block).astype(BF16)
                     )
-        allowed = mask()
+        allowed = allowed_add[...]
+        cos_q, sin_q = cos_sin[0], cos_sin[1]
 
         def heads(g, carry):
             kv_g = kv[l, :, pl.ds(pl.multiple_of(g * 128, 128), 128)]
@@ -521,14 +532,30 @@
             gkv[:, part] = (block * cos_kv - half_turn(block) * sin_kv).astype(BF16)
         op_start((8,), l)
         for at, size in tiles(width, 256):
-            sum_acc[:, at : at + size] = dot_rt(ra[0], wq[at : at + size, :]) + dot_rt(
-                gkv[...], wkv[at : at + size, :]
+            sum_acc[:, at : at + size] = dot_rt(ra[0], wq[at : at + size, :]) + dot(
+                gkv[...], wkv[:, at : at + size]
             )
         go[l] = (gm[...] + norm_back(act[l].astype(F32), gain_attn, 0)).astype(BF16)
         out_start(go.at[l], grads_o, l, 1)
         return carry
 
     lax.fori_loop(0, 2, backward, 0)
+
+    @pl.when(section == 0)
+    def _():
+        for block in range(2):
+
+            @pl.when(jnp.logical_not(in_mine(block)))
+            def _(block=block):
+                in_copy(block, True)[1].wait_send()
+
+    @pl.when(section == 1)
+    def _():
+        for block in range(2):
+
+            @pl.when(jnp.logical_not(in_mine(block)))
+            def _(block=block):
+                in_copy(block, False)[1].wait_send()
 
     op_sent((2, 3, 4, 5, 6, 8), 0)
     for l in range(2):
@@ -546,12 +573,12 @@
             pltpu.make_async_copy(act.at[0], out.at[0, block], out_recv.at[kind, block]).wait()
 
 
-def run_layers(ends, cosines, sines, seg_keys, seg_mine, gains, weights):
+def run_layers(lengths, ends, frequency, gain_attn, gain_ffn, weights):
     micro_count, rows, width = ends.shape[1:]
-    wq, wkv, wo, wg, wu, wd = weights
+    wq, wk, wv, wo, wg, wu, wd = weights
     ff = wg.shape[1]
     keys = RANKS * rows
-    kv_width = wkv.shape[1]
+    kv_width = 2 * wk.shape[0]
     vmem, hbm = pl.BlockSpec(memory_space=pltpu.VMEM), pl.BlockSpec(memory_space=pl.ANY)
     op_rows = 4 * rows
     out = lambda *shape: jax.ShapeDtypeStruct(shape, BF16)
@@ -572,11 +599,11 @@
             out(op_rows, width),
             out(op_rows, 384),
         ],
-        in_specs=[hbm] + [vmem] * 5 + [hbm] * 6,
+        in_specs=[pl.BlockSpec(memory_space=pltpu.SMEM), hbm] + [vmem] * 3 + [hbm] * 7,
         out_specs=[hbm, hbm, vmem] + [hbm] * 9,
         scratch_shapes=[
             pltpu.VMEM(wq.shape, BF16),
-            pltpu.VMEM(wkv.shape, BF16),
+            pltpu.VMEM((kv_width, width), BF16),
             pltpu.VMEM(wo.shape, BF16),
             pltpu.VMEM(wg.shape, BF16),
             pltpu.VMEM(wu.shape, BF16),
@@ -603,7 +630,10 @@
             pltpu.VMEM((keys, kv_width), BF16),
             pltpu.VMEM((2, 3 * rows, kv_width), BF16),
             pltpu.VMEM((rows, kv_width), BF16),
-            dma((6,)),
+            pltpu.VMEM((2, rows, 128), F32),
+            pltpu.VMEM((rows, keys), F32),
+            dma((5,)),
+            dma((2, KEY_VALUE_HEADS)),
             dma((2,)),
             dma((2,)),
             dma((2, 3)),
@@ -620,17 +650,17 @@
             collective_id=1, has_side_effects=True, vmem_limit_bytes=61 * 2**20
         ),
         name="layers",
-    )(ends, cosines, sines, seg_keys, seg_mine, gains, wq, wkv, wo, wg, wu, wd)
+    )(lengths, ends, frequency, gain_attn, gain_ffn, *weights)
 
 
 def sums_kernel(
     gain_sums, nf_h, in_h, gg_h, gu_h, br_h, la_h, ra_h, nr_h, kvg_h,
-    q_o, out_o, kv_o, gain_o, gate_o, up_o, down_o,
+    t_o, gate_o, up_o, down_o,
     stage_a, stage_b, in_v, br_v, gg_v, gu_v, ra_v, kvg_v, nf_t, la_t, nr_t, in_t, gain_t,
     d_out, d_in, d_keep, d1_out, d1_in, d2_out, d2_in,
     f1_out, f1_in, f2_out, f2_in, f_keep, fz_in,
     t1_out, t1_in, t2_out, t2_in, t_keep, tz_in,
-    d_all, f_all, t_all, gate_f, q_f, kv_f, gain_f, down_f,
+    d_all, f_all, t_all,
     load, dz_s, dz_r, d1_s, d1_r, d2_s, d2_r, f1_s, f1_r, f2_s, f2_r, fz_s, fz_r,
     t1_s, t1_r, t2_s, t2_r, tz_s, tz_r, all_s, all_r, pair_r, write,
 ):
@@ -1003,48 +1033,36 @@
     gathers[2].middle()
     gathers[3].middle()
 
-    half_columns = 2 * quarter
-    gathers[0].finish()
-    gathers[1].finish()
-    for core in range(2):
-        columns = slice(512 * core, min(512 * core + 512, width))
-        for h in range(2):
+    writes = []
+
+    def leave(src, dst):
+        writes.append(pltpu.make_async_copy(src, dst, write.at[len(writes)]))
+        writes[-1].start()
+
+    for h in range(2):
+        gathers[h].finish()
+        for core in range(2):
             for spot in range(4):
-                row = h * fine + spot * (fine // 4)
-                down_f[row : row + fine // 4, columns] = d_all[h, core, spot][
-                    :, : columns.stop - columns.start
-                ].astype(F32)
-    writes = [pltpu.make_async_copy(down_f, down_o, write.at[0])]
-    writes[0].start()
+                rows = pl.ds(h * fine + spot * (fine // 4), fine // 4)
+                leave(d_all.at[h, core, spot], down_o.at[rows, pl.ds(core * br_v.shape[1], br_v.shape[1])])
     gathers[4].middle()
     for k in range(2):
         gathers[2 + k].finish()
         for core in range(2):
             for f in range(2):
-                at = core * half_columns + f * quarter
-                columns = slice(at, at + quarter)
-                gate_f[k, :part, columns] = f_all[k, core, 2 * f].astype(F32)
-                gate_f[k, part:, columns] = f_all[k, core, 2 * f + 1, part - shift :, :].astype(F32)
-        writes.append(pltpu.make_async_copy(gate_f.at[k], (gate_o, up_o)[k], write.at[1 + k]))
-        writes[-1].start()
+                columns = pl.ds((2 * core + f) * quarter, quarter)
+                out = (gate_o, up_o)[k]
+                leave(f_all.at[k, core, 2 * f], out.at[pl.ds(0, part), columns])
+                kept = pl.ds(part - shift, per - part)
+                leave(f_all.at[k, core, 2 * f + 1, kept], out.at[pl.ds(part, per - part), columns])
     gathers[4].finish()
     t_rows = part // 2
-    pairs_at = width // 128 * 128 + 128
     for core in range(2):
         for spot in range(4):
             row = spot % 2 * t_rows + spot // 2 * shift
             skip = part - shift if spot == 2 else 0
-            span = slice(row + skip, row + t_rows)
-            q_f[core, span, :] = t_all[core, spot, skip:, :width].astype(F32)
-            kv_f[core, span, :] = t_all[core, spot, skip:, pairs_at:].astype(F32)
-            gain = t_all[core, spot, skip:, pairs_at - 128 : pairs_at].astype(F32)
-            gain_f[span, :] = gain if core == 0 else gain_f[span, :] + gain
-    for i, (src, dst) in enumerate(
-        [(q_f.at[0], q_o), (q_f.at[1], out_o), (kv_f, kv_o), (gain_f, gain_o)]
-    ):
-        writes.append(pltpu.make_async_copy(src, dst, write.at[3 + i]))
-        writes[-1].start()
-
+            kept = pl.ds(skip, t_rows - skip)
+            leave(t_all.at[core, spot, kept], t_o.at[core, pl.ds(row + skip, t_rows - skip)])
     for k in range(3):
         for sub in range(2):
             d_send(k, d_turn(k), sub).wait_send()
@@ -1085,18 +1103,15 @@
     columns = br.shape[1]
     wide_t = width // 128 * 128 + 128 + kvg.shape[1]
     vmem, hbm = pl.BlockSpec(memory_space=pltpu.VMEM), pl.BlockSpec(memory_space=pl.ANY)
-    out = lambda *shape: jax.ShapeDtypeStruct(shape, F32)
+    out = lambda *shape: jax.ShapeDtypeStruct(shape, BF16)
     b = lambda *shape: pltpu.VMEM(shape, BF16)
     f = lambda *shape: pltpu.VMEM(shape, F32)
     sem = lambda *shape: pltpu.SemaphoreType.DMA(shape)
     return pl.pallas_call(
         sums_kernel,
-        out_shape=[
-            out(per, width), out(per, width), out(2, per, kvg.shape[1]), out(per, 128),
-            out(per, ff), out(per, ff), out(deep, width),
-        ],
+        out_shape=[out(2, per, wide_t), out(per, ff), out(per, ff), out(deep, 2 * columns)],
         in_specs=[vmem] + [hbm] * 9,
-        out_specs=[hbm] * 7,
+        out_specs=[hbm] * 4,
         scratch_shapes=[
             b(depth, width), b(depth, width), b(depth, ff), b(depth, columns), b(depth, half), b(depth, half),
             b(depth, width), b(depth, kvg.shape[1]),
@@ -1108,17 +1123,92 @@
             b(RANKS, part, wide_t), b(RANKS, part, wide_t),
             b(RANKS, part // 2, wide_t), b(RANKS, part // 2, wide_t), b(RANKS, part // 2, wide_t), b(5, part // 2, wide_t),
             b(2, 2, 4, fine // 4, columns), b(2, 2, 4, part, quarter), b(2, 4, part // 2, wide_t),
-            f(2, per, ff), f(2, per, width), f(2, per, kvg.shape[1]), f(per, 128), f(deep, width),
             sem(9), sem(3, 2), sem(5, 2), sem(2), sem(2), sem(2), sem(2),
             sem(2, 4), sem(2, 4), sem(2, 4), sem(2, 4), sem(2, 4), sem(2, 5),
             sem(4), sem(4), sem(4), sem(4), sem(4), sem(5),
-            sem(5, 8), sem(5, 4), sem(5, 4), sem(7),
+            sem(5, 8), sem(5, 4), sem(5, 4), sem(40),
         ],
         compiler_params=pltpu.CompilerParams(
             collective_id=2, has_side_effects=True, vmem_limit_bytes=61 * 2**20
         ),
         name="sums",
     )(gain_sums, *operands)
+
+
+def finish_kernel(
+    acts_h, grads_h, t_h, gate_h, up_h, down_h,
+    acts_o, grads_o, q_o, out_o, key_o, value_o, gain_o, gate_o, up_o, down_o,
+    t_v, gate_v, down_v, q_f, kv_f, gate_f, down_f, load, store,
+):
+    width = q_f.shape[2]
+    loads = [
+        pltpu.make_async_copy(h, v, load.at[i])
+        for i, (h, v) in enumerate(
+            [(gate_h, gate_v.at[0]), (up_h, gate_v.at[1]), (down_h, down_v), (t_h, t_v)]
+        )
+    ]
+    stores = [
+        pltpu.make_async_copy(v, h, store.at[i])
+        for i, (v, h) in enumerate(
+            [(acts_h, acts_o), (grads_h, grads_o), (gate_f.at[0], gate_o), (gate_f.at[1], up_o),
+             (down_f, down_o), (q_f.at[0], q_o), (q_f.at[1], out_o), (kv_f.at[0], key_o), (kv_f.at[1], value_o)]
+        )
+    ]
+    for copy in loads + stores[:2]:
+        copy.start()
+    for k in range(2):
+        loads[k].wait()
+        gate_f[k] = gate_v[k].astype(F32)
+        stores[2 + k].start()
+    loads[2].wait()
+    for at, size in tiles(width, 128):
+        down_f[at : at + size, :] = down_v[:, at : at + 128].astype(F32).T[:size]
+    stores[4].start()
+    loads[3].wait()
+    for core in range(2):
+        q_f[core] = t_v[core, :, :width].astype(F32)
+        stores[5 + core].start()
+    pairs_at = width // 128 * 128 + 128
+    half = KEY_VALUE_HEADS // 2 + 1
+    for g in range(KEY_VALUE_HEADS):
+        core = 0 if g < half else 1
+        at = pairs_at + (g - core * (KEY_VALUE_HEADS - half)) * 128
+        block = t_v[core, :, at : at + 128].astype(F32).T
+        kv_f[0, g * HEAD_SIZE : (g + 1) * HEAD_SIZE, :] = block[:HEAD_SIZE]
+        kv_f[1, g * HEAD_SIZE : (g + 1) * HEAD_SIZE, :] = block[HEAD_SIZE:]
+    for copy in stores[7:]:
+        copy.start()
+    tail = slice(pairs_at - 128, pairs_at)
+    both = t_v[0, :, tail].astype(F32) + t_v[1, :, tail].astype(F32)
+    row = width % 128
+    gain_o[...] = both.T[row : row + 8]
+    for copy in stores:
+        copy.wait()
+
+
+def run_finish(acts, grads_in, t_sum, gate, up, down, width):
+    per, ff = gate.shape
+    vmem, hbm = pl.BlockSpec(memory_space=pltpu.VMEM), pl.BlockSpec(memory_space=pl.ANY)
+    out = lambda *shape: jax.ShapeDtypeStruct(shape, F32)
+    kv_rows = KEY_VALUE_HEADS * HEAD_SIZE
+    return pl.pallas_call(
+        finish_kernel,
+        out_shape=[
+            jax.ShapeDtypeStruct(acts.shape, BF16), jax.ShapeDtypeStruct(acts.shape, BF16),
+            out(per, width), out(per, width), out(kv_rows, per), out(kv_rows, per), out(8, per),
+            out(per, ff), out(per, ff), out(width, down.shape[0]),
+        ],
+        in_specs=[hbm] * 6,
+        out_specs=[hbm] * 6 + [vmem] + [hbm] * 3,
+        scratch_shapes=[
+            pltpu.VMEM(t_sum.shape, BF16), pltpu.VMEM((2, per, ff), BF16), pltpu.VMEM(down.shape, BF16),
+            pltpu.VMEM((2, per, width), F32), pltpu.VMEM((2, kv_rows, per), F32),
+            pltpu.VMEM((2, per, ff), F32), pltpu.VMEM((width, down.shape[0]), F32),
+            pltpu.SemaphoreType.DMA((4,)), pltpu.SemaphoreType.DMA((9,)),
+        ],
+        compiler_params=pltpu.CompilerParams(vmem_limit_bytes=40 * 2**20),
+        name="finish",
+    )(acts, grads_in, t_sum, gate, up, down)
 
 
 def sums_by_xla(gain_sums, operands):
@@ -1159,71 +1249,44 @@
     gain_attn,
     gain_ffn,
 ):
-    rows, width = ends.shape[2:]
-    section = lax.axis_index("section")
-    ctx = lax.axis_index("ctx")
-    row_tokens = rows * lax.axis_size("ctx")
-    rank = 2 * section + ctx % 2
-    lengths = lax.dynamic_index_in_dim(doc_lengths, ctx // 2, 0, keepdims=False)[0]
-
-    def place(token_index):
-        segment = jnp.zeros_like(token_index)
-        start = jnp.zeros_like(token_index)
-        finish = jnp.int32(0)
-        for slot in range(lengths.shape[0]):
-            finish = finish + lengths[slot]
-            passed = (token_index >= finish).astype(jnp.int32)
-            segment = segment + passed
-            start = start + passed * lengths[slot]
-        return segment, token_index - start
-
-    seg_keys, _ = place(lax.broadcasted_iota(jnp.int32, (8, row_tokens), 1))
-    seg_mine, token_position = place(
-        rank * rows + lax.broadcasted_iota(jnp.int32, (rows, 128), 0)
-    )
-    lane = lax.broadcasted_iota(jnp.int32, (rows, 128), 1)
+    width = ends.shape[3]
     half = HEAD_SIZE // 2
-    frequency = 10000.0 ** (-2.0 * (lane % half).astype(F32) / HEAD_SIZE)
-    angles = token_position.astype(F32) * frequency
-    cosines = jnp.cos(angles)
-    sines = jnp.where(lane % HEAD_SIZE < half, -1.0, 1.0) * jnp.sin(angles)
-    w_kv = jnp.stack(
-        [
-            key_projection_weight.reshape(width, KEY_VALUE_HEADS, HEAD_SIZE),
-            value_projection_weight.reshape(width, KEY_VALUE_HEADS, HEAD_SIZE),
-        ],
-        axis=2,
-    ).reshape(width, 2 * KEY_VALUE_HEADS * HEAD_SIZE)
-    gains = jnp.concatenate(
-        [jnp.stack([gain_attn, gain_ffn]).astype(F32), jnp.zeros((6, width), F32)]
+    turns = np.float32(10000.0) ** (
+        np.float32(-2.0) * (np.arange(128) % half).astype(np.float32) / np.float32(HEAD_SIZE)
     )
     acts, grads_in, gain_sums, nf, inner, gg, gu, br, la, ra, nr, kvg = run_layers(
+        doc_lengths,
         ends,
-        cosines,
-        sines,
-        seg_keys,
-        seg_mine,
-        gains,
-        (w_query, w_kv, w_out, w_gate, w_up, w_down),
+        jnp.asarray(turns.reshape(1, 128), F32),
+        gain_attn.reshape(1, width),
+        gain_ffn.reshape(1, width),
+        (
+            w_query,
+            key_projection_weight.T,
+            value_projection_weight.T,
+            w_out,
+            w_gate,
+            w_up,
+            w_down.T,
+        ),
     )
-
     operands = (nf, inner, gg, gu, br, la, ra, nr, kvg)
     fits = lax.axis_size("dp") == RANKS and width % 64 == 0 and inner.shape[1] % 1280 == 0
     if fits:
-        grad_query, grad_out, kv_parts, gain_pieces, grad_gate, grad_up, grad_down = run_sums(
-            gain_sums, operands
+        sums = run_sums(gain_sums, operands)
+        acts, grads_in, grad_query, grad_out, grad_key, grad_value, gain_piece, grad_gate, grad_up, grad_down = (
+            run_finish(acts, grads_in, *sums, width)
         )
-        gain_at = width % 128
-        gain_piece = gain_pieces[:, gain_at : gain_at + 2].T
+        grad_key, grad_value, grad_down = grad_key.T, grad_value.T, grad_down.T
     else:
         grad_query, grad_out, kv_parts, gain_piece, grad_gate, grad_up, grad_down = sums_by_xla(
             gain_sums, operands
         )
-    kv_grad = jnp.concatenate([kv_parts[0], kv_parts[1][:, 128:]], axis=1).reshape(
-        -1, KEY_VALUE_HEADS, 2, HEAD_SIZE
-    )
-    grad_key = kv_grad[:, :, 0].reshape(kv_grad.shape[0], -1)
-    grad_value = kv_grad[:, :, 1].reshape(kv_grad.shape[0], -1)
+        kv_grad = jnp.concatenate([kv_parts[0], kv_parts[1][:, 128:]], axis=1).reshape(
+            -1, KEY_VALUE_HEADS, 2, HEAD_SIZE
+        )
+        grad_key = kv_grad[:, :, 0].reshape(kv_grad.shape[0], -1)
+        grad_value = kv_grad[:, :, 1].reshape(kv_grad.shape[0], -1)
     return (
         acts,
         grads_in,

time: 276 us -> 246 us (0.89)
  local copies, waits for them, and re-layouts: 30.2 us -> 8.35 us
  other arithmetic: 6.03 us -> 0 us
    unnamed x24 -> x12, local copies, waits for them, and re-layouts: 20.2 us -> 5.22 us
    pallas_call x1, Pallas kernels: 117 us -> 112 us  [run_layers(): pl.pallas_call(layers_kernel, out_shape=[out(*ends.shape), out(*ends.shap...]
    pallas_call x1 -> x2, Pallas kernels: 120 us -> 125 us  [the longest x1 119 us: run_sums(): pl.pallas_call(sums_kernel, out_shape=[out(2, per, wide_t), out(per, ff),...]
where the time goes in v3:
time: 246 us; the launch traced here: 245 us
  Pallas kernels  236 us (96%)
  local copies, waits for them, and re-layouts  8.35 us (3%)
    pallas_call x1, Pallas kernels, run_sums(): pl.pallas_call(sums_kernel, out_shape=[out(2, per, wide_t), out(per, ff),...  119 us
    pallas_call x1, Pallas kernels, run_layers(): pl.pallas_call(layers_kernel, out_shape=[out(*ends.shape), out(*ends.shap...  112 us
    pallas_call x1, Pallas kernels, run_finish(): pl.pallas_call(finish_kernel, out_shape=[jax.ShapeDtypeStruct(acts.shape,...  5.25 us
    unnamed x12, local copies, waits for them, and re-layouts  5.22 us

profile of v3, /device:TPU:0, one launch (start us, length us, event | category | flops | bytes accessed | tf_op | source)
XLA Modules:
  0.0 245.2 jit_solution(13356226530476226588)
XLA Ops:
  0.6 1.3 reshape.28.gain_a
  1.9 1.3 reshape.29.gain_f
  3.2 111.5 %layers.1 = (bf16[1,2,224,960]{3,2,1,0:T(8,128)(2,1)}, bf16[1,2,224,960]{3,2,1,0:T(8,128)(2,1)}, f32[8,960]{1,0:T(8,128)}, bf16[896,960]{1,0:T(8,128)(2,1)}, bf1...) custom-call(s32[2,1,2]{2,1,0:T(1,128)} %lengths.1, ...), custom_call_target="tpu_custom_call" | custom-call | tf_op jit(solution)/shard_map/layers/pallas_call | solution.py:586
  114.7 0.0 copy-start.4
  114.8 0.0 copy-start.5
  114.8 119.3 %sums.1 = (bf16[2,240,1408]{2,1,0:T(8,128)(2,1)}, bf16[240,2560]{1,0:T(8,128)(2,1)}, bf16[240,2560]{1,0:T(8,128)(2,1)}, bf16[640,1024]{1,0:T(8,128)(2,1)}) custom-call(f32[8,960]{1,0:T(8,128)} %get-tuple-element.39.gain_sums, bf16[896,960]{1,0:T(8,128)(2,1)} %get-tuple-element.40.nf_h, bf16[896,2560]{1,0:T(8,128)(2,1)} %get-tuple-element.41.in_h, ...), custom_call_target="tpu_custom_call" | custom-call | tf_op jit(solution)/shard_map/sums/pallas_call | solution.py:1110
  234.1 0.0 copy-done.4
  234.1 0.0 copy-done.5
  234.1 0.0 copy-start
  234.1 1.3 copy-done
  235.4 0.0 copy-start.1
  235.4 1.3 copy-done.1
  236.8 0.0 copy-start.2
  236.8 1.3 copy-done.2
  238.0 0.0 copy-start.3
  238.0 1.3 copy-done.3
  239.3 5.2 %finish.1 = (bf16[1,2,224,960]{3,2,1,0:T(8,128)(2,1)}, bf16[1,2,224,960]{3,2,1,0:T(8,128)(2,1)}, f32[240,960]{1,0:T(8,128)}, f32[240,960]{1,0:T(8,128)}, f32[320...) custom-call(bf16[1,2,224,960]{3,2,1,0:T(8,128)(2,1)S(1)} %copy-done., ...), custom_call_target="tpu_custom_call" | custom-call | tf_op jit(solution)/shard_map/finish/pallas_call | solution.py:1194
  244.6 0.6 fusion
Async XLA Ops:
  114.7 119.3 %copy-start.4 = (bf16[1,2,224,960]{3,2,1,0:T(8,128)(2,1)S(1)}, bf16[1,2,224,960]{3,2,1,0:T(8,128)(2,1)}, u32[]{:S(2)}) copy-start(bf16[1,2,224,960]{3,2,1,0:T(8,128)(2,1)} %get-tuple-element.37.acts_h) | copy-start | bytes 2580484
  114.8 119.3 %copy-start.5 = (bf16[1,2,224,960]{3,2,1,0:T(8,128)(2,1)S(1)}, bf16[1,2,224,960]{3,2,1,0:T(8,128)(2,1)}, u32[]{:S(2)}) copy-start(bf16[1,2,224,960]{3,2,1,0:T(8,128)(2,1)} %get-tuple-element.38.grads_h) | copy-start | bytes 2580484
  234.1 1.3 copy-start
  235.4 1.3 copy-start.1
  236.8 1.3 copy-start.2
  238.0 1.3 copy-start.3
